TPU v7x, 128 devices: a whole 4x4x4 slice. The times are simulated.
128 devices in a mesh: tile: 16 (over z_lo, x, core), head: 8 (over y, z_hi).
Axes of the slice: x: 4, y: 4, z: 4 (z_hi: 2, z_lo: 2; z = z_hi * 2 + z_lo), core: 2. Of those that a mesh axis runs over, the one named last changes fastest.
Arguments:
- tokens: bfloat16 [4096, 3072], P('tile'), may hold values from -6 to 6
- cotangent: bfloat16 [4096, 3072], P('tile'), may hold values from -6 to 6
- qkv_weight: bfloat16 [3072, 3, 3072], P('tile', None, 'head'), may hold values from -0.109375 to 0.109375
- out_weight: bfloat16 [3072, 3072], P('tile', 'head'), may hold values from -1.75 to 1.75
- slab_of_device: int32 [16], replicated, may hold values from 0 to 15, as said below
- extents: int32 [16, 2], replicated, may hold values from 0 to 1
Outputs:
- output: bfloat16 [4096, 3072], P('tile', 'head')
- grad_tokens: bfloat16 [4096, 3072], P('tile', 'head')
- grad_qkv_weight: float32 [3072, 3, 3072], P('tile', None, 'head')
- grad_out_weight: float32 [3072, 3072], P('tile', 'head')
Inputs may be any that keep to these rules, and one draw needn't show every extreme that they name: slab_of_device[i] equals (r + i) mod 16 for every i, or (r - i) mod 16 for every i, with one r.
All inputs are finite; a program needn't handle non-finite values.
Results may differ from a plain program's by a relative error of at most 0.025.
Values may be sent and summed in bfloat16 or wider, within the bound.
A program may use at most 128 MiB of HBM per device.

v0:
```python
import math

import jax
import jax.numpy as jnp
from jax import lax
from jax.sharding import PartitionSpec as P

HD = 128
TILE_T = 4
TILE_H = 8
TILE_W = 8


epsilon = 1e-06


def unit_rows(raw):
    scale_rows = lax.rsqrt(jnp.mean(raw * raw, axis=-1, keepdims=True) + epsilon)
    return (scale_rows, raw * scale_rows)


def unit_back(grad_unit, scale_rows, unit):
    return scale_rows * (grad_unit - unit * jnp.mean(grad_unit * unit, axis=-1, keepdims=True))


def local(tokens, cotangent, qkv_weight, out_weight, slab_of_device, extents):
    slab_rows = tokens.shape[0]
    width_here = qkv_weight.shape[2]
    heads_here = width_here // HD
    tile_count = lax.axis_size("tile")
    height_tiles = tile_count // TILE_T
    tile_tokens = TILE_H * TILE_W
    width_tiles = slab_rows // tile_tokens
    total_rows = slab_rows * tile_count
    inv_root = 1.0 / math.sqrt(HD)
    my_index = lax.axis_index("tile")
    owners = jnp.arange(tile_count, dtype=jnp.int32)
    my_slab = lax.dynamic_index_in_dim(slab_of_device, my_index, 0, keepdims=False)
    query_height = my_slab % height_tiles
    local_rows = jnp.arange(slab_rows, dtype=jnp.int32)
    query_width = local_rows // tile_tokens
    my_reach = lax.dynamic_slice_in_dim(extents, query_height * width_tiles, width_tiles, 0)
    row_reach = jnp.repeat(my_reach, tile_tokens, axis=0)

    def allowed_for(key_rows):
        owner_hit = (key_rows // slab_rows)[:, None] == owners[None, :]
        key_slab = jnp.sum(jnp.where(owner_hit, slab_of_device[None, :], 0), axis=1)
        near_height = jnp.abs(query_height - key_slab % height_tiles)[None, :] <= row_reach[:, 0:1]
        key_width = key_rows % slab_rows // tile_tokens
        near_width = jnp.abs(query_width[:, None] - key_width[None, :]) <= row_reach[:, 1:2]
        return near_height & near_width

    token_cols = tokens
    proj = jnp.einsum(
        "td,dcf->tcf",
        token_cols,
        lax.all_gather(qkv_weight, "tile", axis=0, tiled=True),
        preferred_element_type=jnp.float32,
    )
    query_raw = proj[:, 0].reshape(slab_rows, heads_here, HD)
    key_raw = proj[:, 1].reshape(slab_rows, heads_here, HD)
    values = proj[:, 2].reshape(slab_rows, heads_here, HD).astype(jnp.bfloat16)
    query_scale, query_unit = unit_rows(query_raw)
    key_scale, key_unit = unit_rows(key_raw)
    query_bf = query_unit.astype(jnp.bfloat16)
    key_bf = key_unit.astype(jnp.bfloat16)
    key_source, value_source = (
        lax.all_gather(key_bf, "tile", axis=0, tiled=True),
        lax.all_gather(values, "tile", axis=0, tiled=True),
    )
    source_rows = jnp.arange(total_rows, dtype=jnp.int32)
    group_size = math.gcd(tile_count, max(1, 1024 // slab_rows))
    step_count = tile_count // group_size
    block_rows = group_size * slab_rows
    key_blocks = key_source.reshape(step_count, block_rows, heads_here, HD)
    value_blocks = value_source.reshape(step_count, block_rows, heads_here, HD)
    row_blocks = source_rows.reshape(step_count, block_rows)

    def exp_scores(key_block, key_rows):
        scores = (
            jnp.einsum("qhd,khd->hqk", query_bf, key_block, preferred_element_type=jnp.float32)
            * inv_root
        )
        return jnp.where(allowed_for(key_rows)[None], jnp.exp(scores), 0.0)

    def forward_step(running, block_parts):
        key_block, value_block, key_rows = block_parts
        weights_exp = exp_scores(key_block, key_rows)
        numerator = running[0] + jnp.einsum(
            "hqk,khd->qhd",
            weights_exp.astype(jnp.bfloat16),
            value_block,
            preferred_element_type=jnp.float32,
        )
        return ((numerator, running[1] + jnp.sum(weights_exp, axis=2)), None)

    start_running = (
        jnp.zeros((slab_rows, heads_here, HD), jnp.float32),
        jnp.zeros((heads_here, slab_rows), jnp.float32),
    )
    numerator, denominator = lax.scan(
        forward_step, start_running, (key_blocks, value_blocks, row_blocks)
    )[0]
    context = numerator / jnp.transpose(denominator)[:, :, None]
    attended = context.astype(jnp.bfloat16).reshape(slab_rows, width_here)
    out_partial = jnp.einsum(
        "tf,of->to",
        attended,
        lax.all_gather(out_weight, "tile", axis=0, tiled=True),
        preferred_element_type=jnp.float32,
    )
    output = lax.psum_scatter(
        out_partial.astype(jnp.bfloat16), "head", scatter_dimension=1, tiled=True
    )
    grad_cols = cotangent
    grad_attended = jnp.dot(
        grad_cols,
        lax.all_gather(out_weight, "tile", axis=0, tiled=True),
        preferred_element_type=jnp.float32,
    )
    grad_attended = grad_attended.astype(jnp.bfloat16)
    grad_cols = cotangent
    grad_out_weight = lax.psum_scatter(
        jnp.einsum("to,tf->of", grad_cols, attended, preferred_element_type=jnp.float32).astype(
            jnp.bfloat16
        ),
        "tile",
        scatter_dimension=0,
        tiled=True,
    ).astype(jnp.float32)
    grad_heads = grad_attended.reshape(slab_rows, heads_here, HD)
    row_delta = jnp.transpose(jnp.sum(grad_heads.astype(jnp.float32) * context, axis=-1))

    def backward_step(grad_query_unit, block_parts):
        key_block, value_block, key_rows = block_parts
        weights_exp = exp_scores(key_block, key_rows)
        softmax_probs = weights_exp / denominator[:, :, None]
        grad_probs = jnp.einsum(
            "qhd,khd->hqk", grad_heads, value_block, preferred_element_type=jnp.float32
        )
        grad_scores = (softmax_probs * (grad_probs - row_delta[:, :, None])).astype(jnp.bfloat16)
        grad_query_unit = (
            grad_query_unit
            + jnp.einsum("hqk,khd->qhd", grad_scores, key_block, preferred_element_type=jnp.float32)
            * inv_root
        )
        key_term = (
            jnp.einsum("hqk,qhd->khd", grad_scores, query_bf, preferred_element_type=jnp.float32)
            * inv_root
        )
        value_term = jnp.einsum(
            "hqk,qhd->khd",
            softmax_probs.astype(jnp.bfloat16),
            grad_heads,
            preferred_element_type=jnp.float32,
        )
        return (grad_query_unit, (key_term, value_term))

    grad_query_unit, block_terms = lax.scan(
        backward_step,
        jnp.zeros((slab_rows, heads_here, HD), jnp.float32),
        (key_blocks, value_blocks, row_blocks),
    )
    key_terms = block_terms[0].reshape(tile_count, slab_rows, heads_here, HD)
    value_terms = block_terms[1].reshape(tile_count, slab_rows, heads_here, HD)
    grad_key_unit, grad_values = (
        lax.psum_scatter(
            key_terms.reshape(total_rows, heads_here, HD).astype(jnp.bfloat16),
            "tile",
            scatter_dimension=0,
            tiled=True,
        ).astype(jnp.float32),
        lax.psum_scatter(
            value_terms.reshape(total_rows, heads_here, HD).astype(jnp.bfloat16),
            "tile",
            scatter_dimension=0,
            tiled=True,
        ).astype(jnp.float32),
    )
    grad_query = unit_back(grad_query_unit, query_scale, query_unit)
    grad_key = unit_back(grad_key_unit, key_scale, key_unit)
    grad_proj = jnp.stack([grad_query, grad_key, grad_values], axis=1)
    grad_proj = grad_proj.reshape(slab_rows, 3, width_here).astype(jnp.bfloat16)
    token_partial = jnp.einsum(
        "tcf,dcf->td",
        grad_proj,
        lax.all_gather(qkv_weight, "tile", axis=0, tiled=True),
        preferred_element_type=jnp.float32,
    )
    grad_tokens = lax.psum_scatter(
        token_partial.astype(jnp.bfloat16), "head", scatter_dimension=1, tiled=True
    )
    token_cols = tokens
    grad_qkv_weight = lax.psum_scatter(
        jnp.einsum("td,tcf->dcf", token_cols, grad_proj, preferred_element_type=jnp.float32).astype(
            jnp.bfloat16
        ),
        "tile",
        scatter_dimension=0,
        tiled=True,
    ).astype(jnp.float32)
    return (output, grad_tokens, grad_qkv_weight, grad_out_weight)


def solution(mesh):
    placed = (
        P("tile", None),
        P("tile", None),
        P("tile", None, "head"),
        P("tile", "head"),
        P(),
        P(),
    )
    return jax.shard_map(
        local,
        mesh=mesh,
        in_specs=placed,
        out_specs=(
            P("tile", "head"),
            P("tile", "head"),
            P("tile", None, "head"),
            P("tile", "head"),
        ),
        check_vma=False,
    )
```

profile of v0, /device:TPU:1, one launch (start us, length us, event | category | flops | bytes accessed | tf_op | source)
XLA Modules:
  0.0 703.9 jit_solution(15592001648123776104)
XLA Ops:
  8.7 50.6 %all-gather.5.cloned.1.call-done = bf16[3072,3,384]{2,0,1:T(8,128)(2,1)} async-done(((bf16[192,3,384]{2,0,1:T(8,128)(2,1)}), bf16[3072,3,384]{2,0,1:T(8,128)(2,1)}) %all-gather.5.cloned.1.call-update) | async-done | bytes 7077904 | tf_op jit(solution)/shard_map/all_gather | solution.py:57
  59.3 5.2 fusion.64
  67.9 1.7 slice.49
  69.6 1.7 copy.80
  75.5 20.7 %all-gather.11.cloned.1.call-done = bf16[3072,384]{1,0:T(8,128)(2,1)} async-done(((bf16[192,384]{1,0:T(8,128)(2,1)}), bf16[3072,384]{1,0:T(8,128)(2,1)}) %all-gather.11.cloned.1.call-update) | async-done | bytes 2359312 | tf_op jit(solution)/shard_map/all_gather | solution.py:109
  96.3 3.3 convolution_convert_fusion.3
  100.8 1.2 copy.84
  102.3 37.5 %all-gather.9.cloned.1.call-done = bf16[4096,3,128]{0,2,1:T(8,128)(2,1)} async-done(((bf16[256,3,128]{0,2,1:T(8,128)(2,1)}), bf16[4096,3,128]{0,2,1:T(8,128)(2,1)}) %all-gather.9.cloned.1.call-update) | async-done | bytes 3145744 | tf_op jit(solution)/shard_map/all_gather | solution.py:68
  139.7 4.7 copy.83
  144.4 3.8 copy.86
  148.2 35.0 %all-gather.7.cloned.1.call-done = bf16[4096,3,128]{0,2,1:T(8,128)(2,1)} async-done(((bf16[256,3,128]{0,2,1:T(8,128)(2,1)}), bf16[4096,3,128]{0,2,1:T(8,128)(2,1)}) %all-gather.7.cloned.1.call-update) | async-done | bytes 3145744 | tf_op jit(solution)/shard_map/all_gather | solution.py:69
  183.3 4.7 copy.81
  187.9 33.1 %while.34 = (s32[]{:T(128)}, f32[256,3,128]{0,2,1:T(8,128)S(1)}, f32[3,256]{1,0:T(4,128)S(1)}, bf16[4,1024,3,128]{3,1,0,2:T(8,128)(2,1)}, s32[]{:T(128)}, /*inde...) while((s32[]{:T(128)}, f32[256,3,128]{0,2,1:T(8,128)S(1)}, ...), condition=%wide.region_5.6_spmd.clone, body=%wide.region_2.5_spmd.clone.sunk | while | flops 408985344 | bytes 9699544 | solution.py:101
  189.6 3.6 fusion.120
  193.2 3.0 fusion.121
  197.9 3.6 fusion.120
  201.5 3.0 fusion.121
  206.2 3.6 fusion.120
  209.8 3.0 fusion.121
  214.5 3.6 fusion.120
  218.0 3.0 fusion.121
  221.8 54.1 %while.35 = (s32[]{:T(128)}, f32[256,3,128]{0,2,1:T(8,128)}, bf16[4,1024,3,128]{3,1,0,2:T(8,128)(2,1)}, bf16[4,1024,3,128]{3,1,0,2:T(8,128)(2,1)}, bf16[4,1024,3...) while((s32[]{:T(128)}, f32[256,3,128]{0,2,1:T(8,128)}, ...), condition=%wide.region_10.11_spmd.clone, body=%wide.region_8.10_spmd.clone.sunk | while | flops 1014242304 | bytes 72149936 | solution.py:159
  223.5 1.9 fusion.135
  225.5 1.7 copy-done.1
  227.1 1.7 fusion.136
  228.9 2.5 fusion.137
  231.4 1.5 bitcast_dynamic-update-slice_fusion.4
  233.6 1.7 copy-done.9
  236.9 1.9 fusion.135
  238.9 1.7 copy-done.1
  240.6 1.7 fusion.136
  242.3 2.6 fusion.137
  244.9 1.5 bitcast_dynamic-update-slice_fusion.4
  247.2 1.7 copy-done.9
  250.5 1.9 fusion.135
  252.5 1.7 copy-done.1
  254.2 1.7 fusion.136
  255.9 2.6 fusion.137
  258.5 1.5 bitcast_dynamic-update-slice_fusion.4
  260.7 1.7 copy-done.9
  264.1 1.9 fusion.135
  266.0 1.7 copy-done.1
  267.7 1.7 fusion.136
  269.4 2.6 fusion.137
  272.0 1.5 bitcast_dynamic-update-slice_fusion.4
  274.3 1.7 copy-done.9
  276.0 4.8 copy.94
  281.7 2.7 convolution_convert_fusion.2
  284.4 1.6 copy.107
  286.0 3.6 fusion.61
  289.6 4.4 copy.113
  294.4 42.9 %reduce-scatter.17.cloned.1.call-done = bf16[256,3,128]{2,0,1:T(8,128)(2,1)} async-done(((bf16[4096,3,128]{2,0,1:T(8,128)(2,1)}), bf16[256,3,128]{2,0,1:T(8,128)(2,1)}) %reduce-scatter.17.cloned.1.call-update) | async-done | bytes 196624 | tf_op jit(solution)/shard_map/reduce_scatter | solution.py:173
  338.6 64.8 %reduce-scatter.15.cloned.1.call-done = bf16[256,3,128]{0,2,1:T(8,128)(2,1)} async-done(((bf16[4096,3,128]{0,2,1:T(8,128)(2,1)}), bf16[256,3,128]{0,2,1:T(8,128)(2,1)}) %reduce-scatter.15.cloned.1.call-update) | async-done | bytes 196624 | tf_op jit(solution)/shard_map/reduce_scatter | solution.py:167
  406.2 5.4 fusion.62
  411.6 1.6 copy.109
  413.2 5.9 convolution_convert_fusion
  419.1 10.1 %copy.115 = bf16[3072,1152]{1,0:T(8,128)(2,1)} copy(bf16[3072,1152]{0,1:T(8,128)(2,1)} %bitcast.175) | data formatting | bytes 14155776
  429.2 53.5 %reduce-scatter.19.cloned.1.call-done = bf16[384,256]{1,0:T(8,128)(2,1)} async-done(((bf16[3072,256]{1,0:T(8,128)(2,1)}), bf16[384,256]{1,0:T(8,128)(2,1)}) %reduce-scatter.19.cloned.1.call-update) | async-done | bytes 196624
  482.7 1.7 copy.108
  484.4 60.6 %reduce-scatter.25.cloned.1.call-done = bf16[192,384]{1,0:T(8,128)(2,1)} async-done(((bf16[3072,384]{1,0:T(8,128)(2,1)}), bf16[192,384]{1,0:T(8,128)(2,1)}) %reduce-scatter.25.cloned.1.call-update) | async-done | bytes 147472
  546.9 77.3 %reduce-scatter.21.cloned.1.call-done = bf16[384,256]{1,0:T(8,128)(2,1)} async-done(((bf16[3072,256]{1,0:T(8,128)(2,1)}), bf16[384,256]{1,0:T(8,128)(2,1)}) %reduce-scatter.21.cloned.1.call-update) | async-done | bytes 196624
  624.2 1.7 copy.110
  625.9 68.7 %reduce-scatter.23.cloned.1.call-done = bf16[192,1152]{1,0:T(8,128)(2,1)} async-done(((bf16[3072,1152]{1,0:T(8,128)(2,1)}), bf16[192,1152]{1,0:T(8,128)(2,1)}) %reduce-scatter.23.cloned.1.call-update) | async-done | bytes 442384
  694.7 1.2 copy.116
  (187 shorter events, 34.1 us)
Async XLA Ops:
  7.2 52.2 %copy-start = (bf16[256,3072]{1,0:T(8,128)(2,1)S(1)}, bf16[256,3072]{1,0:T(8,128)(2,1)}, u32[]{:S(2)}) copy-start(bf16[256,3072]{1,0:T(8,128)(2,1)} %param.10) | copy-start | bytes 4718596
  7.2 52.2 %all-gather.5.cloned.1.call-start = ((), (), s32[]{:S(2)}) async-start(), calls=%async_computation.6 | async-start | bytes 7520256 | tf_op jit(solution)/shard_map/all_gather | solution.py:57
  7.9 88.4 %all-gather.11.cloned.1.call-start = ((), (), s32[]{:S(2)}) async-start(), calls=%async_computation.9 | async-start | bytes 2506752 | tf_op jit(solution)/shard_map/all_gather | solution.py:109
  8.7 131.1 %all-gather.9.cloned.1.call-start = ((), (), s32[]{:S(2)}) async-start(), calls=%async_computation.8 | async-start | bytes 3342336 | tf_op jit(solution)/shard_map/all_gather | solution.py:68
  64.5 1.3 copy-start.12
  64.6 6.8 copy-start.16
  64.6 31.7 %copy-start.11 = (bf16[256,3072]{1,0:T(8,128)(2,1)S(1)}, bf16[256,3072]{1,0:T(8,128)(2,1)}, u32[]{:S(2)}) copy-start(bf16[256,3072]{1,0:T(8,128)(2,1)} %param.11) | copy-start | bytes 4718596
  67.0 32.6 %copy-start.4 = (f32[256,1,384]{0,2,1:T(8,128)}, f32[256,1,384]{0,2,1:T(8,128)S(1)}, u32[]{:S(2)}) copy-start(f32[256,1,384]{0,2,1:T(8,128)S(1)} %copy.82) | copy-start | bytes 1179652
  67.8 115.4 %all-gather.7.cloned.1.call-start = ((), (), s32[]{:S(2)}) async-start(), calls=%async_computation.7 | async-start | bytes 3342336 | tf_op jit(solution)/shard_map/all_gather | solution.py:69
  71.3 266.0 %reduce-scatter.17.cloned.1.call-start = ((), (), s32[]{:S(2)}) async-start(), calls=%async_computation.11 | async-start | bytes 3342336 | tf_op jit(solution)/shard_map/reduce_scatter | solution.py:173
  102.0 42.4 %copy-start.6 = (f32[256,1,384]{0,2,1:T(8,128)}, f32[256,1,384]{0,2,1:T(8,128)S(1)}, u32[]{:S(2)}) copy-start(f32[256,1,384]{0,2,1:T(8,128)S(1)} %copy.84) | copy-start | bytes 1179652
  102.1 42.4 %copy-start.14 = (f32[256,3]{0,1:T(4,128)}, f32[256,3]{0,1:T(4,128)S(1)}, u32[]{:S(2)}) copy-start(f32[256,3]{0,1:T(4,128)S(1)} %add_rsqrt_fusion) | copy-start | bytes 9220
  148.2 39.7 %copy-start.13 = (f32[256,3,128]{0,2,1:T(8,128)S(1)}, f32[256,3,128]{0,2,1:T(8,128)}, u32[]{:S(2)}) copy-start(f32[256,3,128]{0,2,1:T(8,128)} %custom-call) | copy-start | bytes 1179652
  148.2 39.7 %copy-start.17 = (s32[16]{0:T(128)S(1)}, s32[16]{0:T(128)}, u32[]{:S(2)}) copy-start(s32[16]{0:T(128)} %param.14) | copy-start | bytes 196
  221.8 3.6 copy-start.18
  225.5 1.7 copy-start.1
  228.9 4.0 copy-start.2
  228.9 4.0 copy-start.8
  232.8 2.4 copy-start.19
  233.6 1.7 copy-start.9
  235.3 3.6 copy-start.18
  238.9 1.7 copy-start.1
  242.3 4.1 copy-start.2
  242.3 4.1 copy-start.8
  246.4 2.4 copy-start.19
  247.2 1.7 copy-start.9
  248.8 3.6 copy-start.18
  252.5 1.7 copy-start.1
  255.9 4.1 copy-start.2
  255.9 4.1 copy-start.8
  260.0 2.4 copy-start.19
  260.7 1.7 copy-start.9
  262.4 3.6 copy-start.18
  266.0 1.7 copy-start.1
  269.4 4.1 copy-start.2
  269.4 4.1 copy-start.8
  273.5 2.4 copy-start.19
  274.3 1.7 copy-start.9
  276.0 127.4 %reduce-scatter.15.cloned.1.call-start = ((), (), s32[]{:S(2)}) async-start(), calls=%async_computation.10 | async-start | bytes 3342336 | tf_op jit(solution)/shard_map/reduce_scatter | solution.py:167
  280.8 0.9 copy-start.10
  280.8 201.9 %reduce-scatter.19.cloned.1.call-start = ((), (), s32[]{:S(2)}) async-start(), calls=%async_computation.12 | async-start | bytes 1769472
  286.0 259.0 %reduce-scatter.25.cloned.1.call-start = ((), (), s32[]{:S(2)}) async-start(), calls=%async_computation.15 | async-start | bytes 2506752
  289.6 4.5 copy-start.3
  289.6 4.5 copy-start.7
  289.6 4.5 copy-start.15
  294.0 109.3 %copy-start.5 = (f32[256,1,384]{0,2,1:T(8,128)S(1)}, f32[256,1,384]{0,2,1:T(8,128)}, u32[]{:S(2)}) copy-start(f32[256,1,384]{0,2,1:T(8,128)} %copy-done.4) | copy-start | bytes 1179652
  294.0 330.1 %reduce-scatter.21.cloned.1.call-start = ((), (), s32[]{:S(2)}) async-start(), calls=%async_computation.13 | async-start | bytes 1769472
  413.2 281.5 %reduce-scatter.23.cloned.1.call-start = ((), (), s32[]{:S(2)}) async-start(), calls=%async_computation.14 | async-start | bytes 7520256
Sparse Core Ops, SparseCore 0:
  9.7 49.6 all-gather.4
  61.0 35.1 all-gather.10
  98.5 41.2 all-gather.8
  141.8 41.4 all-gather.6
  276.1 61.1 reduce-scatter.16
  339.6 63.7 reduce-scatter.14
  407.1 75.5 reduce-scatter.18
  485.1 59.8 reduce-scatter.24
  548.7 75.3 reduce-scatter.20
  626.5 68.1 reduce-scatter.22
where the time goes:
time: 709 us; the launch traced here: 704 us
  waiting for transfers between devices  513 us (72%)
  matrix products  86 us (12%)
  local copies, waits for them, and re-layouts  69.5 us (10%)
  other arithmetic  17.7 us (2%)
  between operations  16.4 us (2%)
    unnamed x14, waiting for transfers between devices  262 us
    reduce_scatter x1, waiting for transfers between devices, local(): lax.psum_scatter(key_terms.reshape(total_rows, heads_here, HD).astype(jnp...  64.8 us
    all_gather x1, waiting for transfers between devices, local(): lax.all_gather(qkv_weight, 'tile', axis=0, tiled=True)  50.6 us
    reduce_scatter x1, waiting for transfers between devices, local(): lax.psum_scatter(value_terms.reshape(total_rows, heads_here, HD).astype(j...  42.9 us
    all_gather x1, waiting for transfers between devices, local(): lax.all_gather(key_bf, 'tile', axis=0, tiled=True)  37.5 us
    all_gather x1, waiting for transfers between devices, local(): lax.all_gather(values, 'tile', axis=0, tiled=True)  35 us
    unnamed x41, local copies, waits for them, and re-layouts  30.5 us
    dot_general x8, matrix products, exp_scores(): jnp.einsum('qhd,khd->hqk', query_bf, key_block, preferred_element_type=jn...  22 us
  transfers between devices with their start and end apart: 10, of which 10 were waited for; matrix products, arithmetic and copies ran while one was open for 11% of the time, Pallas kernels for 0%

commit v1 on v0

v1 whole, which is shorter than its diff:
```python
import math

import jax
import jax.numpy as jnp
from jax import lax
from jax.experimental import pallas as pl
from jax.experimental.pallas import tpu as pltpu
from jax.sharding import PartitionSpec as P

MESH = pl.DeviceIdType.MESH
HD = 128
NH = 3
ROWS = 256
WID = NH * HD
D = 3072
OWN = 192
EPS = 1e-06
INV_ROOT = 1.0 / math.sqrt(HD)
EXP2_SCALE = INV_ROOT * math.log2(math.e)
BF = jnp.bfloat16
F32 = jnp.float32
GATHER_COPIES = 17
SCATTER_COPIES = 7


def dot(a, b):
    return jnp.dot(a, b, preferred_element_type=F32)


def dot_nt(a, b):
    return lax.dot_general(a, b, (((1,), (1,)), ((), ())), preferred_element_type=F32)


def at_tile(z, x, c):
    return z * 8 + x * 2 + c


class Place:
    def __init__(self):
        t = lax.axis_index("tile")
        self.me = t
        self.z, self.x, self.c = t // 8, (t // 2) % 4, t % 2
        self.xr, self.xl, self.xo = (self.x + 1) % 4, (self.x + 3) % 4, (self.x + 2) % 4
        self.right = at_tile(self.z, self.xr, self.c)
        self.left = at_tile(self.z, self.xl, self.c)
        self.across = at_tile(1 - self.z, self.x, self.c)
        self.sib = at_tile(self.z, self.x, 1 - self.c)


class Gather:
    def __init__(self, place, buf, send, recv):
        self.p, self.buf, self.send, self.recv = place, buf, send, recv
        self.half_rows = buf.shape[1] // 2
        self.sent = []

    def slot(self, t):
        return self.buf.at[t]

    def half(self, t, i):
        return self.buf.at[t, pl.ds(i * self.half_rows, self.half_rows)]

    def copy(self, k, ref, dev):
        return pltpu.make_async_remote_copy(
            src_ref=ref, dst_ref=ref, send_sem=self.send.at[k], recv_sem=self.recv.at[k],
            device_id={"tile": dev}, device_id_type=MESH)

    def go(self, k, ref, dev):
        c = self.copy(k, ref, dev)
        c.start()
        self.sent.append(c)

    def got(self, k, ref):
        self.copy(k, ref, self.p.sib).wait_recv()

    def start(self):
        p = self.p
        me = self.slot(p.me)
        self.go(0, me, p.right)
        self.go(1, me, p.left)
        self.go(2, me, p.across)
        self.go(3, me, p.sib)

    def step_across(self):
        p = self.p
        s = self.slot(p.across)
        self.got(2, s)
        self.go(4, s, p.right)
        self.go(5, s, p.left)
        self.go(6, s, p.sib)

    def step_sides(self):
        p = self.p
        for i, zz in enumerate((p.z, 1 - p.z)):
            tl, tr = at_tile(zz, p.xl, p.c), at_tile(zz, p.xr, p.c)
            self.got((0, 4)[i], self.slot(tl))
            self.go(7 + i, self.half(tl, 0), p.right)
            self.got((1, 5)[i], self.slot(tr))
            self.go(9 + i, self.half(tr, 1), p.left)
            self.go(11 + i, self.slot(tl), p.sib)
            self.go(13 + i, self.slot(tr), p.sib)

    def step_opposite(self):
        p = self.p
        for i, zz in enumerate((p.z, 1 - p.z)):
            to = at_tile(zz, p.xo, p.c)
            self.got(7 + i, self.half(to, 0))
            self.got(9 + i, self.half(to, 1))
            self.go(15 + i, self.slot(to), p.sib)

    def sib_own(self):
        p = self.p
        self.got(3, self.slot(p.sib))

    def sib_across(self):
        p = self.p
        self.got(6, self.slot(at_tile(1 - p.z, p.x, 1 - p.c)))

    def sib_sides(self):
        p = self.p
        for i, zz in enumerate((p.z, 1 - p.z)):
            self.got(11 + i, self.slot(at_tile(zz, p.xl, 1 - p.c)))
            self.got(13 + i, self.slot(at_tile(zz, p.xr, 1 - p.c)))

    def sib_opposite(self):
        p = self.p
        for i, zz in enumerate((p.z, 1 - p.z)):
            self.got(15 + i, self.slot(at_tile(zz, p.xo, 1 - p.c)))

    def finish(self):
        for c in self.sent:
            c.wait_send()


class Scatter:
    def __init__(self, axis, ring, pair, devices, parts, far, near, last, send, recv):
        self.axis, self.ring, self.pair = axis, ring, pair
        self.right, self.left, self.across = devices
        self.parts, self.far, self.near, self.last = parts, far, near, last
        self.send, self.recv = send, recv
        self.rr, self.rl, self.ro = (ring + 1) % 4, (ring + 3) % 4, (ring + 2) % 4
        rows = parts.shape[2]
        self.lo, self.hi = pl.ds(0, rows // 2), pl.ds(rows // 2, rows // 2)
        self.sent = []

    def copy(self, k, src, dst, dev):
        return pltpu.make_async_remote_copy(
            src_ref=src, dst_ref=dst, send_sem=self.send.at[k], recv_sem=self.recv.at[k],
            device_id={self.axis: dev}, device_id_type=MESH)

    def go(self, k, src, dst, dev):
        c = self.copy(k, src, dst, dev)
        c.start()
        self.sent.append(c)

    def got(self, k, dst):
        self.copy(k, dst, dst, self.right).wait_recv()

    def add(self, ring, rows, got):
        for i in range(2):
            self.parts[ring, i, rows] = (
                self.parts[ring, i, rows].astype(F32) + got[i].astype(F32)).astype(BF)

    def start_far(self):
        self.go(0, self.parts.at[self.ro, :, self.lo], self.far.at[0], self.right)
        self.go(1, self.parts.at[self.ro, :, self.hi], self.far.at[1], self.left)

    def start_near(self):
        self.go(2, self.parts.at[self.rr, :, self.hi], self.near.at[0, :, self.hi], self.right)
        self.go(3, self.parts.at[self.rl, :, self.lo], self.near.at[1, :, self.lo], self.left)

    def step_near(self):
        self.got(0, self.far.at[0])
        self.add(self.rr, self.lo, self.far.at[0])
        self.go(4, self.parts.at[self.rr, :, self.lo], self.near.at[0, :, self.lo], self.right)
        self.got(1, self.far.at[1])
        self.add(self.rl, self.hi, self.far.at[1])
        self.go(5, self.parts.at[self.rl, :, self.hi], self.near.at[1, :, self.hi], self.left)

    def total(self, pair):
        return (self.parts[self.ring, pair].astype(F32) + self.near[0, pair].astype(F32)
                + self.near[1, pair].astype(F32))

    def step_pair(self):
        self.got(2, self.near.at[0, :, self.hi])
        self.got(3, self.near.at[1, :, self.lo])
        self.got(4, self.near.at[0, :, self.lo])
        self.got(5, self.near.at[1, :, self.hi])
        other = 1 - self.pair
        self.parts[self.ring, other] = self.total(other).astype(BF)
        self.go(6, self.parts.at[self.ring, other], self.last, self.across)

    def result(self):
        self.got(6, self.last)
        return self.total(self.pair) + self.last[...].astype(F32)

    def finish(self):
        for c in self.sent:
            c.wait_send()


def kernel(tok_hbm, cot_hbm, w_hbm, wo_hbm, slab, ext,
           out_ref, gtok_ref, gqkv_ref, gout_ref,
           w, wo, kv, tok, cot, tok_t, tok_sib, cot_t, cot_sib, wexp, mask,
           proj, q, qt, g, gt, num, den, delta, dq, att, gp, dkv_sum,
           dkv_out, dkv_parts, dkv_far, dkv_near, dkv_last,
           gq_parts, gq_far, gq_near, gq_last,
           go_parts, go_far, go_near, go_last,
           hd_parts, ho_far, ho_near, ho_last, ht_far, ht_near, ht_last,
           load_sem, gat_send, gat_recv, sca_send, sca_recv, sib_send, sib_recv, dkv_send, dkv_recv):
    p = Place()
    hd = lax.axis_index("head")
    hy, hz = hd // 2, hd % 2
    head_devices = (((hy + 1) % 4) * 2 + hz, ((hy + 3) % 4) * 2 + hz, hy * 2 + 1 - hz)
    lane_devices = (p.right, p.left, p.across)

    loads = [pltpu.make_async_copy(a, b, load_sem.at[i]) for i, (a, b) in enumerate((
        (w_hbm, w.at[p.me]), (wo_hbm, wo.at[p.me]), (tok_hbm, tok), (cot_hbm, cot)))]
    for c in loads:
        c.start()

    barrier = pltpu.get_barrier_semaphore()
    for dev in (p.right, p.left, p.across, p.sib):
        pl.semaphore_signal(barrier, inc=1, device_id={"tile": dev}, device_id_type=MESH)
    for dev in head_devices:
        pl.semaphore_signal(barrier, inc=1, device_id={"head": dev}, device_id_type=MESH)
    pl.semaphore_wait(barrier, 7)

    sent = []

    def to_sibling(k, src, dst):
        c = pltpu.make_async_remote_copy(
            src_ref=src, dst_ref=dst, send_sem=sib_send.at[k], recv_sem=sib_recv.at[k],
            device_id={"tile": p.sib}, device_id_type=MESH)
        c.start()
        sent.append(c)
        return c

    gather_w = Gather(p, w, gat_send.at[0], gat_recv.at[0])
    gather_o = Gather(p, wo, gat_send.at[1], gat_recv.at[1])
    gather_kv = Gather(p, kv, gat_send.at[2], gat_recv.at[2])
    scatter = lambda i, parts, far, near, last: Scatter(
        "tile", p.x, p.z, lane_devices, parts, far, near, last, sca_send.at[i], sca_recv.at[i])
    head_scatter = lambda i, parts, far, near, last: Scatter(
        "head", hy, hz, head_devices, parts, far, near, last, sca_send.at[i], sca_recv.at[i])
    sum_dkv = scatter(0, dkv_parts, dkv_far, dkv_near, dkv_last)
    sum_gq = scatter(1, gq_parts, gq_far, gq_near, gq_last)
    sum_go = scatter(2, go_parts, go_far, go_near, go_last)
    sum_out = head_scatter(3, hd_parts, ho_far, ho_near, ho_last)
    sum_tok = head_scatter(4, hd_parts, ht_far, ht_near, ht_last)

    loads[0].wait()
    gather_w.start()

    height = lax.rem(slab[p.me], 4)
    near_height = lax.rem(slab[p.sib], 4)
    far_height = lax.rem(slab[at_tile(p.z, p.xr, 1 - p.c)], 4)
    key_width = lax.broadcasted_iota(jnp.int32, (64, ROWS), 1) // 64
    for qw in range(4):
        reach_h = ext[height * 4 + qw, 0]
        reach_w = ext[height * 4 + qw, 1]
        near_w = jnp.where(jnp.abs(key_width - qw) <= reach_w, 1.0, 0.0)
        for m, other in enumerate((height, near_height, far_height)):
            gap = jnp.full((64, ROWS), jnp.abs(height - other), jnp.int32)
            mask[m, qw * 64:(qw + 1) * 64] = jnp.where(gap <= reach_h, near_w, 0.0)

    loads[2].wait()
    loads[3].wait()

    def turn(src, dst):
        def body(j, carry):
            cols = pl.ds(pl.multiple_of(j * 384, 384), 384)
            dst[j] = src[:, cols].T.reshape(2, OWN, ROWS)
            return carry
        lax.fori_loop(0, 8, body, 0)

    turn(tok, tok_t)
    tok_swap = to_sibling(0, tok_t.at[:, 1 - p.c], tok_sib)

    def project(z, x, first=False):
        j = z * 4 + x
        t = tok[:, pl.ds(pl.multiple_of(j * 384, 384), 384)]
        for i in range(3):
            chunk = w[pl.ds(2 * j, 2), i * OWN:(i + 1) * OWN, :].reshape(2 * OWN, WID)
            if first:
                proj[i] = dot(t, chunk)
            else:
                proj[i] += dot(t, chunk)

    gather_w.step_across()
    turn(cot, cot_t)
    cot_swap = to_sibling(1, cot_t.at[:, 1 - p.c], cot_sib)
    gather_w.sib_own()
    project(p.z, p.x, True)
    gather_w.sib_across()
    project(1 - p.z, p.x)
    gather_w.step_sides()
    loads[1].wait()
    gather_o.start()
    gather_w.sib_sides()
    for zz in (p.z, 1 - p.z):
        project(zz, p.xl)
        project(zz, p.xr)
    gather_w.step_opposite()
    gather_o.step_across()
    gather_w.sib_opposite()
    for zz in (p.z, 1 - p.z):
        project(zz, p.xo)

    def scale_of(raw):
        return lax.rsqrt(jnp.mean(raw * raw, axis=-1, keepdims=True) + EPS)

    for h in range(NH):
        hs = slice(h * HD, (h + 1) * HD)
        raw = proj[1, :, hs]
        kv[p.me, :, hs] = (raw * scale_of(raw)).astype(BF)
    kv[p.me, :, WID:] = proj[2].astype(BF)
    gather_kv.start()
    for h in range(NH):
        hs = slice(h * HD, (h + 1) * HD)
        raw = proj[0, :, hs]
        unit = (raw * scale_of(raw)).astype(BF)
        q[:, hs] = unit
        qt[h] = unit.T

    def forward(t, m, i, first=False):
        for h in range(NH):
            hs = slice(h * HD, (h + 1) * HD)
            vs = slice(WID + h * HD, WID + (h + 1) * HD)
            scores = dot_nt(q[:, hs], kv[t, :, hs])
            we = jnp.exp2(scores * EXP2_SCALE) * mask[m]
            wexp[i, h] = we
            part = we[:, :HD] + we[:, HD:]
            val = dot(we.astype(BF), kv[t, :, vs])
            if first:
                den[h] = part
                num[:, hs] = val
            else:
                den[h] += part
                num[:, hs] += val

    def loop2(fn):
        lax.fori_loop(0, 2, lambda i, carry: (fn(i), carry)[1], 0)

    gather_o.step_sides()
    forward(p.me, 0, 0, True)
    gather_kv.step_across()
    gather_kv.sib_own()
    forward(p.sib, 1, 2)
    gather_o.step_opposite()
    forward(p.across, 0, 1)
    gather_kv.sib_across()
    forward(at_tile(1 - p.z, p.x, 1 - p.c), 1, 3)
    gather_o.sib_own()
    gather_o.sib_across()
    gather_o.sib_sides()
    gather_o.sib_opposite()

    def grad_att(j, acc):
        cols = pl.ds(pl.multiple_of(j * 384, 384), 384)
        return acc + dot(cot[:, cols], wo[pl.ds(2 * j, 2)].reshape(2 * OWN, WID))

    g[...] = lax.fori_loop(0, 8, grad_att, jnp.zeros((ROWS, WID), F32)).astype(BF)
    for h in range(NH):
        gt[h] = g[:, h * HD:(h + 1) * HD].T
    gather_kv.step_sides()
    gather_kv.sib_sides()

    def sides(i):
        zz = (p.z + i) % 2
        forward(at_tile(zz, p.xl, 1 - p.c), 2, 4 + 2 * i)
        forward(at_tile(zz, p.xr, 1 - p.c), 2, 5 + 2 * i)

    loop2(sides)
    gather_kv.step_opposite()
    loop2(lambda i: forward(at_tile((p.z + i) % 2, p.xo, p.c), 0, 8 + i))
    gather_kv.sib_opposite()
    loop2(lambda i: forward(at_tile((p.z + i) % 2, p.xo, 1 - p.c), 1, 10 + i))

    for h in range(NH):
        hs = slice(h * HD, (h + 1) * HD)
        inverse = 1.0 / jnp.sum(den[h], axis=-1, keepdims=True)
        context = num[:, hs] * inverse
        att[0, :, hs] = context.astype(BF)
        row = jnp.sum(g[:, hs].astype(F32) * context, axis=-1, keepdims=True)
        delta[h] = jnp.broadcast_to(row, (ROWS, HD))
        den[h] = jnp.broadcast_to(inverse, (ROWS, HD))
    att_swap = to_sibling(2, att.at[0], att.at[1])

    def backward(t, i, dst, first=False, adding=False):
        for h in range(NH):
            hs = slice(h * HD, (h + 1) * HD)
            vs = slice(WID + h * HD, WID + (h + 1) * HD)
            grad = dot_nt(g[:, hs], kv[t, :, vs])
            inverse, row = den[h], delta[h]
            probs, ds = [], []
            for part in range(2):
                cs = slice(part * HD, (part + 1) * HD)
                pr = wexp[i, h, :, cs] * inverse
                ds.append((pr * (grad[:, cs] - row)).astype(BF))
                probs.append(pr.astype(BF))
            probs = jnp.concatenate(probs, axis=1)
            ds = jnp.concatenate(ds, axis=1)
            term = dot(ds, kv[t, :, hs])
            if first:
                dq[:, hs] = term
            else:
                dq[:, hs] += term
            dk = dot(qt[h], ds) * INV_ROOT
            dv = dot(gt[h], probs)
            if adding:
                dk = dk + dst[hs].astype(F32)
                dv = dv + dst[vs].astype(F32)
            dst[hs] = dk.astype(BF)
            dst[vs] = dv.astype(BF)

    def swap_copy(x, z, k):
        return pltpu.make_async_remote_copy(
            src_ref=dkv_out.at[x, z], dst_ref=dkv_parts.at[x, z], send_sem=dkv_send.at[k],
            recv_sem=dkv_recv.at[k], device_id={"tile": p.sib}, device_id_type=MESH)

    def swap(x, z, k):
        c = swap_copy(x, z, k)
        c.start()
        sent.append(c)

    def out_part(j, carry):
        hd_parts[j // 2, j % 2] = dot_nt(att[0], wo[pl.ds(2 * j, 2)].reshape(2 * OWN, WID)).astype(BF)
        return carry

    def opposite_sib(i):
        zz = (p.z + i) % 2
        backward(at_tile(zz, p.xo, 1 - p.c), 10 + i, dkv_out.at[p.xo, zz])

    dq[...] = jnp.zeros_like(dq)
    loop2(opposite_sib)
    swap(p.xo, p.z, 0)
    swap(p.xo, 1 - p.z, 1)
    lax.fori_loop(0, 8, out_part, 0)
    sum_out.start_far()
    sum_out.start_near()

    def sides_sib(i):
        zz = (p.z + i) % 2
        backward(at_tile(zz, p.xl, 1 - p.c), 4 + 2 * i, dkv_out.at[p.xl, zz])
        backward(at_tile(zz, p.xr, 1 - p.c), 5 + 2 * i, dkv_out.at[p.xr, zz])

    loop2(sides_sib)
    for i, zz in enumerate((p.z, 1 - p.z)):
        swap(p.xl, zz, 2 + i)
        swap(p.xr, zz, 4 + i)
    for i, zz in enumerate((p.z, 1 - p.z)):
        swap_copy(p.xo, zz, i).wait_recv()

    def opposite_own(i):
        zz = (p.z + i) % 2
        backward(at_tile(zz, p.xo, p.c), 8 + i, dkv_parts.at[p.xo, zz], adding=True)

    loop2(opposite_own)
    sum_dkv.start_far()
    for i, zz in enumerate((p.z, 1 - p.z)):
        swap_copy(p.xl, zz, 2 + i).wait_recv()
        swap_copy(p.xr, zz, 4 + i).wait_recv()
    sum_dkv.start_near()

    def own_sib(i):
        zz = (p.z + i) % 2
        backward(at_tile(zz, p.x, 1 - p.c), 2 + i, dkv_out.at[p.x, zz])

    loop2(own_sib)
    for i, zz in enumerate((p.z, 1 - p.z)):
        swap(p.x, zz, 6 + i)
    sum_out.step_near()
    sum_dkv.step_near()
    for i, zz in enumerate((p.z, 1 - p.z)):
        swap_copy(p.x, zz, 6 + i).wait_recv()

    def own_own(i):
        zz = (p.z + i) % 2
        backward(at_tile(zz, p.x, p.c), i, dkv_parts.at[p.x, zz], adding=True)

    loop2(own_own)

    att_swap.wait_recv()
    cot_swap.wait_recv()

    def out_grad(j, carry):
        go_parts[j % 4, j // 4] = (dot(cot_t[j, p.c], att[0]) + dot(cot_sib[j], att[1])).astype(BF)
        return carry

    lax.fori_loop(0, 8, out_grad, 0)
    sum_go.start_far()
    sum_go.start_near()

    def unit_back(grad, raw):
        scale = scale_of(raw)
        unit = raw * scale
        return scale * (grad - unit * jnp.mean(grad * unit, axis=-1, keepdims=True))

    for h in range(NH):
        hs = slice(h * HD, (h + 1) * HD)
        gp[0, 0, :, hs] = unit_back(dq[:, hs] * INV_ROOT, proj[0, :, hs]).astype(BF)
    sum_out.step_pair()
    sum_dkv.step_pair()
    sum_go.step_near()
    out_ref[...] = sum_out.result().astype(BF)
    dkv_sum[...] = sum_dkv.result()
    for h in range(NH):
        hs = slice(h * HD, (h + 1) * HD)
        vs = slice(WID + h * HD, WID + (h + 1) * HD)
        gp[0, 1, :, hs] = unit_back(dkv_sum[hs].T, proj[1, :, hs]).astype(BF)
        gp[0, 2, :, hs] = dkv_sum[vs].T.astype(BF)
    gp_swap = to_sibling(3, gp.at[0], gp.at[1])
    sum_go.step_pair()

    tok_swap.wait_recv()
    gp_swap.wait_recv()

    def qkv_grad(j):
        for i in range(3):
            gq_parts[j % 4, j // 4, i * OWN:(i + 1) * OWN] = (
                dot(tok_t[j, p.c], gp[0, i]) + dot(tok_sib[j], gp[1, i])).astype(BF)

    loop2(lambda i: qkv_grad(i * 4 + p.xo))
    sum_gq.start_far()
    loop2(lambda i: qkv_grad(i * 4 + p.xr))
    loop2(lambda i: qkv_grad(i * 4 + p.xl))
    sum_gq.start_near()
    sum_out.finish()

    def tok_part(j, carry):
        acc = dot_nt(gp[0, 0], w[pl.ds(2 * j, 2), 0:OWN, :].reshape(2 * OWN, WID))
        for i in range(1, 3):
            acc += dot_nt(gp[0, i], w[pl.ds(2 * j, 2), i * OWN:(i + 1) * OWN, :].reshape(2 * OWN, WID))
        hd_parts[j // 2, j % 2] = acc.astype(BF)
        return carry

    lax.fori_loop(0, 8, tok_part, 0)
    sum_tok.start_far()
    sum_tok.start_near()
    loop2(lambda i: qkv_grad(i * 4 + p.x))
    sum_gq.step_near()
    sum_tok.step_near()
    gout_ref[...] = sum_go.result()
    sum_tok.step_pair()
    sum_gq.step_pair()
    gtok_ref[...] = sum_tok.result().astype(BF)
    gqkv_ref[...] = sum_gq.result()

    for s in (gather_w, gather_o, gather_kv, sum_dkv, sum_gq, sum_go, sum_tok):
        s.finish()
    for c in sent:
        c.wait_send()


def lane_bufs(rows, cols):
    return [pltpu.VMEM((2, 2, rows // 2, cols), BF), pltpu.VMEM((2, 2, rows, cols), BF),
            pltpu.VMEM((rows, cols), BF)]


def local(tokens, cotangent, qkv_weight, out_weight, slab_of_device, extents):
    w = jnp.transpose(qkv_weight, (1, 0, 2)).reshape(3 * OWN, WID)
    vm = lambda *shape, dtype=BF: pltpu.VMEM(shape, dtype)
    dma = lambda *shape: pltpu.SemaphoreType.DMA(shape)
    scratch = [
        vm(16, 3 * OWN, WID), vm(16, OWN, WID), vm(16, ROWS, 2 * WID), vm(ROWS, D), vm(ROWS, D),
        vm(8, 2, OWN, ROWS), vm(8, OWN, ROWS), vm(8, 2, OWN, ROWS), vm(8, OWN, ROWS),
        vm(12, NH, ROWS, ROWS, dtype=F32), vm(3, ROWS, ROWS, dtype=F32),
        vm(3, ROWS, WID, dtype=F32), vm(ROWS, WID), vm(NH, HD, ROWS), vm(ROWS, WID), vm(NH, HD, ROWS),
        vm(ROWS, WID, dtype=F32), vm(NH, ROWS, HD, dtype=F32), vm(NH, ROWS, HD, dtype=F32),
        vm(ROWS, WID, dtype=F32), vm(2, ROWS, WID), vm(2, 3, ROWS, WID), vm(2 * WID, ROWS, dtype=F32),
        vm(4, 2, 2 * WID, ROWS), vm(4, 2, 2 * WID, ROWS), *lane_bufs(2 * WID, ROWS),
        vm(4, 2, 3 * OWN, WID), *lane_bufs(3 * OWN, WID),
        vm(4, 2, OWN, WID), *lane_bufs(OWN, WID),
        vm(4, 2, ROWS, WID), *lane_bufs(ROWS, WID), *lane_bufs(ROWS, WID),
        dma(4), dma(3, GATHER_COPIES), dma(3, GATHER_COPIES), dma(5, SCATTER_COPIES), dma(5, SCATTER_COPIES),
        dma(4), dma(4), dma(8), dma(8),
    ]
    any_spec = pl.BlockSpec(memory_space=pl.ANY)
    smem = pl.BlockSpec(memory_space=pltpu.SMEM)
    vmem = pl.BlockSpec(memory_space=pltpu.VMEM)
    output, grad_tokens, grad_qkv, grad_out = pl.pallas_call(
        kernel,
        out_shape=(
            jax.ShapeDtypeStruct((ROWS, WID), BF), jax.ShapeDtypeStruct((ROWS, WID), BF),
            jax.ShapeDtypeStruct((3 * OWN, WID), F32), jax.ShapeDtypeStruct((OWN, WID), F32)),
        in_specs=[any_spec] * 4 + [smem] * 2,
        out_specs=(vmem,) * 4,
        scratch_shapes=scratch,
        compiler_params=pltpu.CompilerParams(
            collective_id=0, has_side_effects=True, vmem_limit_bytes=64 * 1024 * 1024),
        cost_estimate=pl.CostEstimate(flops=20_000_000_000, bytes_accessed=10_000_000, transcendentals=2_400_000),
        name="sublayer",
    )(tokens, cotangent, w, out_weight, slab_of_device, extents)
    grad_qkv = jnp.transpose(grad_qkv.reshape(3, OWN, WID), (1, 0, 2))
    return output, grad_tokens, grad_qkv, grad_out


def solution(mesh):
    return jax.shard_map(
        local, mesh=mesh,
        in_specs=(P("tile", None), P("tile", None), P("tile", None, "head"), P("tile", "head"), P(None), P(None, None)),
        out_specs=(P("tile", "head"), P("tile", "head"), P("tile", None, "head"), P("tile", "head")),
        check_vma=False)
```

time: 709 us -> 180 us (0.25)
  waiting for transfers between devices: 513 us -> 0 us
  Pallas kernels: 0 us -> 171 us
  matrix products: 86 us -> 0 us
  local copies, waits for them, and re-layouts: 69.5 us -> 7.5 us
  other arithmetic: 17.7 us -> 0 us
  between operations: 16.4 us -> 0.65 us
    unnamed x14 -> x0, waiting for transfers between devices: 262 us -> none
    pallas_call x0 -> x1, Pallas kernels: none -> 171 us  [local(): pl.pallas_call(kernel, out_shape=(jax.ShapeDtypeStruct((ROWS, WID), BF),...]
    all_gather x4 -> x0, waiting for transfers between devices: 144 us -> none  [the longest x1 50.6 us: local(): lax.all_gather(qkv_weight, 'tile', axis=0, tiled=True)]
    reduce_scatter x2 -> x0, waiting for transfers between devices: 108 us -> none  [the longest x1 64.8 us: local(): lax.psum_scatter(key_terms.reshape(total_rows, heads_here, HD).astype(jnp...]
    dot_general x34 -> x0, matrix products: 86 us -> none  [the longest x8 22 us: exp_scores(): jnp.einsum('qhd,khd->hqk', query_bf, key_block, preferred_element_type=jn...]
    unnamed x41 -> x7, local copies, waits for them, and re-layouts: 30.5 us -> 7.5 us
    while x48 -> x0, local copies, waits for them, and re-layouts: 13.4 us -> none
    all_gather x2 -> x0, local copies, waits for them, and re-layouts: 9.34 us -> none  [the longest x1 4.67 us: local(): lax.all_gather(key_bf, 'tile', axis=0, tiled=True)]
  transfers between devices with their start and end apart: 10 -> 0, of which waited for: 10 -> 0; matrix products, arithmetic and copies ran while one was open for 11% -> 0% of each run, Pallas kernels for 0% -> 0%
where the time goes in v1:
time: 180 us
  Pallas kernels  171 us (95%)
  local copies, waits for them, and re-layouts  7.5 us (4%)
    pallas_call x1, Pallas kernels, local(): pl.pallas_call(kernel, out_shape=(jax.ShapeDtypeStruct((ROWS, WID), BF),...  171 us
    unnamed x7, local copies, waits for them, and re-layouts  7.5 us

profile of v1, /device:TPU:1, one launch (start us, length us, event | category | flops | bytes accessed | tf_op | source)
XLA Modules:
  0.0 179.6 jit_solution(3430394384093004779)
XLA Ops:
  0.6 1.4 copy.10.ext
  2.0 171.5 %sublayer.1 = (bf16[256,384]{1,0:T(8,128)(2,1)}, bf16[256,384]{1,0:T(8,128)(2,1)}, f32[576,384]{1,0:T(8,128)}, f32[192,384]{1,0:T(8,128)}) custom-call(bf16[256,3072]{1,0:T(8,128)(2,1)} %tok_hbm.1, bf16[256,3072]{1,0:T(8,128)(2,1)} %cot_hbm.1, bf16[576,384]{1,0:T(8,128)(2,1)} %bitcast.7, bf16[192,384]{1,0:T(8,128)(2,1)} %wo_hbm.1, s32[16]{0:T(128)} %slab.1, ...), custom_call_target="tpu_custom_call" | custom-call | flops 20000000000 | bytes 10000000 | tf_op jit(solution)/shard_map/sublayer/pallas_call | solution.py:581
  173.5 0.0 copy-start
  173.5 1.7 copy.15
  175.1 1.6 copy.16
  176.8 2.1 %copy.17 = f32[192,3,384]{2,0,1:T(8,128)} copy(f32[192,3,384]{2,0,1:T(8,128)} %bitcast.6) | data formatting | bytes 1769472
  178.9 0.0 copy-done
  178.9 0.7 copy.18
Async XLA Ops:
  173.5 5.4 %copy-start = (f32[192,384]{1,0:T(8,128)S(1)}, f32[192,384]{1,0:T(8,128)}, u32[]{:S(2)}) copy-start(f32[192,384]{1,0:T(8,128)} %get-tuple-element.19) | copy-start | bytes 884740

commit v2 on v1

v2 whole, which is shorter than its diff:
```python
import math

import jax
import jax.numpy as jnp
from jax import lax
from jax.experimental import pallas as pl
from jax.experimental.pallas import tpu as pltpu
from jax.sharding import PartitionSpec as P

MESH = pl.DeviceIdType.MESH
HD = 128
NH = 3
ROWS = 256
WID = NH * HD
D = 3072
OWN = 192
EPS = 1e-06
INV_ROOT = 1.0 / math.sqrt(HD)
EXP2_SCALE = INV_ROOT * math.log2(math.e)
BF = jnp.bfloat16
F32 = jnp.float32
GATHER_COPIES = 32
SCATTER_COPIES = 17
QKV_FIRST, OUT_FIRST, KV_FIRST, DKV_FIRST = 320, 112, 144, 432


def dot(a, b):
    return jnp.dot(a, b, preferred_element_type=F32)


def dot_nt(a, b):
    return lax.dot_general(a, b, (((1,), (1,)), ((), ())), preferred_element_type=F32)


def at_tile(z, x, c):
    return z * 8 + x * 2 + c


class Place:
    def __init__(self):
        t = lax.axis_index("tile")
        self.me = t
        self.z, self.x, self.c = t // 8, (t // 2) % 4, t % 2
        self.xr, self.xl, self.xo = (self.x + 1) % 4, (self.x + 3) % 4, (self.x + 2) % 4
        self.right = at_tile(self.z, self.xr, self.c)
        self.left = at_tile(self.z, self.xl, self.c)
        self.across = at_tile(1 - self.z, self.x, self.c)
        self.sib = at_tile(self.z, self.x, 1 - self.c)


def split_rows(rows, first):
    def halves(start, size, up):
        half = size // 32 * 16 + (16 if up and size % 32 else 0)
        return pl.ds(start, size), (pl.ds(start, half), pl.ds(start + half, size - half))
    a, ah = halves(0, first, True)
    b, bh = halves(first, rows - first, False)
    return a, ah, b, bh


class Gather:
    def __init__(self, place, buf, first, send, recv):
        self.p, self.buf, self.send, self.recv = place, buf, send, recv
        self.a, self.ah, self.b, self.bh = split_rows(buf.shape[1], first)
        self.sent = []

    def copy(self, k, ref, dev):
        return pltpu.make_async_remote_copy(
            src_ref=ref, dst_ref=ref, send_sem=self.send.at[k], recv_sem=self.recv.at[k],
            device_id={"tile": dev}, device_id_type=MESH)

    def go(self, k, t, rows, dev):
        c = self.copy(k, self.buf.at[t, rows], dev)
        c.start()
        self.sent.append(c)

    def got(self, k, t, rows):
        self.copy(k, self.buf.at[t, rows], self.p.sib).wait_recv()

    def start(self):
        p = self.p
        self.go(0, p.me, self.a, p.across)
        self.go(1, p.me, self.b, p.right)
        self.go(2, p.me, self.b, p.left)
        self.go(3, p.me, self.a, p.right)
        self.go(4, p.me, self.a, p.left)
        self.go(5, p.me, self.b, p.across)
        c = self.copy(6, self.buf.at[p.me], p.sib)
        c.start()
        self.sent.append(c)

    def step_across(self):
        p = self.p
        self.got(0, p.across, self.a)
        self.go(7, p.across, self.a, p.right)
        self.go(8, p.across, self.a, p.left)
        self.go(9, p.across, self.a, p.sib)

    def step_sides(self):
        p = self.p
        self.got(1, p.left, self.b)
        self.go(10, p.left, self.bh[0], p.right)
        self.go(11, p.left, self.b, p.across)
        self.got(2, p.right, self.b)
        self.go(12, p.right, self.bh[1], p.left)
        self.go(13, p.right, self.b, p.across)
        self.got(3, p.left, self.a)
        self.go(14, p.left, self.ah[0], p.right)
        self.got(4, p.right, self.a)
        self.go(15, p.right, self.ah[1], p.left)
        self.go(16, p.left, self.b, p.sib)
        self.go(17, p.right, self.b, p.sib)
        self.go(18, p.left, self.a, p.sib)
        self.go(19, p.right, self.a, p.sib)
        self.got(5, p.across, self.b)
        self.go(20, p.across, self.b, p.sib)

    def step_sides_across(self):
        p = self.p
        zl, zr = at_tile(1 - p.z, p.xl, p.c), at_tile(1 - p.z, p.xr, p.c)
        self.got(7, zl, self.a)
        self.go(21, zl, self.ah[0], p.right)
        self.got(8, zr, self.a)
        self.go(22, zr, self.ah[1], p.left)
        self.go(23, zl, self.a, p.sib)
        self.go(24, zr, self.a, p.sib)

    def step_opposite(self):
        p = self.p
        zl, zr = at_tile(1 - p.z, p.xl, p.c), at_tile(1 - p.z, p.xr, p.c)
        to = at_tile(p.z, p.xo, p.c)
        self.got(10, to, self.bh[0])
        self.got(12, to, self.bh[1])
        self.go(25, to, self.b, p.across)
        self.got(14, to, self.ah[0])
        self.got(15, to, self.ah[1])
        c = self.copy(26, self.buf.at[to], p.sib)
        c.start()
        self.sent.append(c)
        self.got(11, zl, self.b)
        self.go(27, zl, self.b, p.sib)
        self.got(13, zr, self.b)
        self.go(28, zr, self.b, p.sib)

    def step_last(self):
        p = self.p
        zo = at_tile(1 - p.z, p.xo, p.c)
        self.got(21, zo, self.ah[0])
        self.got(22, zo, self.ah[1])
        self.go(29, zo, self.a, p.sib)
        self.got(25, zo, self.b)
        self.go(30, zo, self.b, p.sib)

    def sib_own(self):
        self.copy(6, self.buf.at[self.p.sib], self.p.sib).wait_recv()

    def sib_across(self):
        p = self.p
        t = at_tile(1 - p.z, p.x, 1 - p.c)
        self.got(9, t, self.a)
        self.got(20, t, self.b)

    def sib_sides(self):
        p = self.p
        tl, tr = at_tile(p.z, p.xl, 1 - p.c), at_tile(p.z, p.xr, 1 - p.c)
        self.got(16, tl, self.b)
        self.got(17, tr, self.b)
        self.got(18, tl, self.a)
        self.got(19, tr, self.a)

    def sib_sides_across(self):
        p = self.p
        zl, zr = at_tile(1 - p.z, p.xl, 1 - p.c), at_tile(1 - p.z, p.xr, 1 - p.c)
        self.got(23, zl, self.a)
        self.got(24, zr, self.a)
        self.got(27, zl, self.b)
        self.got(28, zr, self.b)

    def sib_opposite(self):
        p = self.p
        self.copy(26, self.buf.at[at_tile(p.z, p.xo, 1 - p.c)], p.sib).wait_recv()

    def sib_last(self):
        p = self.p
        zo = at_tile(1 - p.z, p.xo, 1 - p.c)
        self.got(29, zo, self.a)
        self.got(30, zo, self.b)

    def finish(self):
        for c in self.sent:
            c.wait_send()


class Scatter:
    def __init__(self, axis, ring, pair, devices, parts, first, bufs, send, recv):
        self.axis, self.ring, self.pair = axis, ring, pair
        self.right, self.left, self.across = devices
        self.parts = parts
        self.far, self.near, self.last = bufs[:3]
        self.zed, self.far_b, self.near_b = bufs[3:] if len(bufs) > 3 else (None, None, None)
        self.send, self.recv = send, recv
        self.rr, self.rl, self.ro = (ring + 1) % 4, (ring + 3) % 4, (ring + 2) % 4
        self.a, self.ah, self.b, self.bh = split_rows(parts.shape[2], first)
        self.first = first
        self.bl = [pl.ds(h.start - first, h.size) for h in self.bh]
        self.sent = []

    def copy(self, k, src, dst, dev):
        return pltpu.make_async_remote_copy(
            src_ref=src, dst_ref=dst, send_sem=self.send.at[k], recv_sem=self.recv.at[k],
            device_id={self.axis: dev}, device_id_type=MESH)

    def go(self, k, src, dst, dev):
        c = self.copy(k, src, dst, dev)
        c.start()
        self.sent.append(c)

    def got(self, k, dst):
        self.copy(k, dst, dst, self.right).wait_recv()

    def add(self, ring, pair, rows, got):
        self.parts[ring, pair, rows] = (
            self.parts[ring, pair, rows].astype(F32) + got.astype(F32)).astype(BF)

    def start_z(self, k, ring):
        self.go(k, self.parts.at[ring, 1 - self.pair, self.b], self.zed.at[ring], self.across)

    def got_z(self, k, ring):
        self.got(k, self.zed.at[ring])

    def start_far(self):
        if self.zed is not None:
            self.start_z(0, self.ro)
        for i, dev in enumerate((self.right, self.left)):
            self.go(4 + i, self.parts.at[self.ro, :, self.ah[i]], self.far.at[i, :, pl.ds(0, self.ah[i].size)], dev)

    def start_near(self):
        if self.zed is not None:
            self.start_z(1, self.rr)
            self.start_z(2, self.rl)
        self.go(6, self.parts.at[self.rr, :, self.ah[1]], self.near.at[0, :, self.ah[1]], self.right)
        self.go(7, self.parts.at[self.rl, :, self.ah[0]], self.near.at[1, :, self.ah[0]], self.left)

    def start_own(self):
        self.start_z(3, self.ring)

    def step_far_b(self):
        self.got_z(0, self.ro)
        self.add(self.ro, self.pair, self.b, self.zed[self.ro])
        for i, dev in enumerate((self.right, self.left)):
            self.go(10 + i, self.parts.at[self.ro, self.pair, self.bh[i]], self.far_b.at[i, pl.ds(0, self.bh[i].size)], dev)

    def step_near(self):
        for i, (ring, dev) in enumerate(((self.rr, self.right), (self.rl, self.left))):
            got = self.far.at[i, :, pl.ds(0, self.ah[i].size)]
            self.got(4 + i, got)
            for z in range(2):
                self.add(ring, z, self.ah[i], got[z])
            self.go(8 + i, self.parts.at[ring, :, self.ah[i]], self.near.at[i, :, self.ah[i]], dev)

    def step_near_b(self):
        for i, (ring, dev) in enumerate(((self.rr, self.right), (self.rl, self.left))):
            self.got_z(1 + i, ring)
            self.add(ring, self.pair, self.b, self.zed[ring])
            j = 1 - i
            self.go(12 + i, self.parts.at[ring, self.pair, self.bh[j]], self.near_b.at[i, self.bl[j]], dev)
        for i, (ring, dev) in enumerate(((self.rr, self.right), (self.rl, self.left))):
            got = self.far_b.at[i, pl.ds(0, self.bh[i].size)]
            self.got(10 + i, got)
            self.add(ring, self.pair, self.bh[i], got[...])
            self.go(14 + i, self.parts.at[ring, self.pair, self.bh[i]], self.near_b.at[i, self.bl[i]], dev)

    def total(self, pair):
        return (self.parts[self.ring, pair, self.a].astype(F32) + self.near[0, pair].astype(F32)
                + self.near[1, pair].astype(F32))

    def step_pair(self):
        for i in range(2):
            self.got(6 + i, self.near.at[i, :, self.ah[1 - i]])
            self.got(8 + i, self.near.at[i, :, self.ah[i]])
        other = 1 - self.pair
        self.parts[self.ring, other, self.a] = self.total(other).astype(BF)
        self.go(16, self.parts.at[self.ring, other, self.a], self.last, self.across)

    def result(self, out):
        if self.zed is not None:
            self.got_z(3, self.ring)
            for i in range(2):
                self.got(12 + i, self.near_b.at[i, self.bl[1 - i]])
                self.got(14 + i, self.near_b.at[i, self.bl[i]])
            out[self.b] = (
                (self.parts[self.ring, self.pair, self.b].astype(F32) + self.zed[self.ring].astype(F32))
                + (self.near_b[0].astype(F32) + self.near_b[1].astype(F32))).astype(out.dtype)
        self.got(16, self.last)
        out[self.a] = (self.total(self.pair) + self.last[...].astype(F32)).astype(out.dtype)

    def finish(self):
        for c in self.sent:
            c.wait_send()


def kernel(tok_hbm, cot_hbm, w_hbm, wo_hbm, slab, ext,
           out_ref, gtok_ref, gqkv_ref, gout_ref,
           w, wo, kv, tok, cot, tok_t, tok_sib, cot_t, cot_sib, wexp, mask,
           proj, q, qt, g, gt, num, den, delta, dq, att, gp, dkv_sum,
           dkv_out, dkv_parts, dkv_far, dkv_near, dkv_last, dkv_zed, dkv_far_b, dkv_near_b,
           gq_parts, gq_far, gq_near, gq_last, gq_zed, gq_far_b, gq_near_b,
           go_parts, go_far, go_near, go_last, go_zed, go_far_b, go_near_b,
           hd_parts, ho_far, ho_near, ho_last, ht_far, ht_near, ht_last,
           load_sem, gat_send, gat_recv, sca_send, sca_recv, sib_send, sib_recv, dkv_send, dkv_recv):
    p = Place()
    hd = lax.axis_index("head")
    hy, hz = hd // 2, hd % 2
    head_devices = (((hy + 1) % 4) * 2 + hz, ((hy + 3) % 4) * 2 + hz, hy * 2 + 1 - hz)
    lane_devices = (p.right, p.left, p.across)

    loads = [pltpu.make_async_copy(a, b, load_sem.at[i]) for i, (a, b) in enumerate((
        (w_hbm, w.at[p.me]), (wo_hbm, wo.at[p.me]), (tok_hbm, tok), (cot_hbm, cot)))]
    for c in loads:
        c.start()

    barrier = pltpu.get_barrier_semaphore()
    for dev in (p.right, p.left, p.across, p.sib):
        pl.semaphore_signal(barrier, inc=1, device_id={"tile": dev}, device_id_type=MESH)
    for dev in head_devices:
        pl.semaphore_signal(barrier, inc=1, device_id={"head": dev}, device_id_type=MESH)
    pl.semaphore_wait(barrier, 7)

    sent = []

    def to_sibling(k, src, dst):
        c = pltpu.make_async_remote_copy(
            src_ref=src, dst_ref=dst, send_sem=sib_send.at[k], recv_sem=sib_recv.at[k],
            device_id={"tile": p.sib}, device_id_type=MESH)
        c.start()
        sent.append(c)
        return c

    gather_w = Gather(p, w, QKV_FIRST, gat_send.at[0], gat_recv.at[0])
    gather_o = Gather(p, wo, OUT_FIRST, gat_send.at[1], gat_recv.at[1])
    gather_kv = Gather(p, kv, KV_FIRST, gat_send.at[2], gat_recv.at[2])
    scatter = lambda i, parts, first, *bufs: Scatter(
        "tile", p.x, p.z, lane_devices, parts, first, bufs, sca_send.at[i], sca_recv.at[i])
    head_scatter = lambda i, parts, *bufs: Scatter(
        "head", hy, hz, head_devices, parts, ROWS, bufs, sca_send.at[i], sca_recv.at[i])
    sum_dkv = scatter(0, dkv_parts, DKV_FIRST, dkv_far, dkv_near, dkv_last, dkv_zed, dkv_far_b, dkv_near_b)
    sum_gq = scatter(1, gq_parts, QKV_FIRST, gq_far, gq_near, gq_last, gq_zed, gq_far_b, gq_near_b)
    sum_go = scatter(2, go_parts, OUT_FIRST, go_far, go_near, go_last, go_zed, go_far_b, go_near_b)
    sum_out = head_scatter(3, hd_parts, ho_far, ho_near, ho_last)
    sum_tok = head_scatter(4, hd_parts, ht_far, ht_near, ht_last)

    loads[0].wait()
    gather_w.start()

    height = lax.rem(slab[p.me], 4)
    near_height = lax.rem(slab[p.sib], 4)
    far_height = lax.rem(slab[at_tile(p.z, p.xr, 1 - p.c)], 4)
    key_width = lax.broadcasted_iota(jnp.int32, (64, ROWS), 1) // 64
    for qw in range(4):
        reach_h = ext[0, height * 4 + qw]
        reach_w = ext[1, height * 4 + qw]
        near_w = jnp.where(jnp.abs(key_width - qw) <= reach_w, 1.0, 0.0)
        for m, other in enumerate((height, near_height, far_height)):
            gap = jnp.full((64, ROWS), jnp.abs(height - other), jnp.int32)
            mask[m, qw * 64:(qw + 1) * 64] = jnp.where(gap <= reach_h, near_w, 0.0)

    loads[2].wait()
    loads[3].wait()

    def turn(src, dst):
        def body(j, carry):
            cols = pl.ds(pl.multiple_of(j * 384, 384), 384)
            dst[j] = src[:, cols].T.reshape(2, OWN, ROWS)
            return carry
        lax.fori_loop(0, 8, body, 0)

    turn(tok, tok_t)
    tok_swap = to_sibling(0, tok_t.at[:, 1 - p.c], tok_sib)
    turn(cot, cot_t)
    cot_swap = to_sibling(1, cot_t.at[:, 1 - p.c], cot_sib)

    def project(z, x, first=False):
        j = z * 4 + x
        t = tok[:, pl.ds(pl.multiple_of(j * 384, 384), 384)]
        for i in range(3):
            chunk = w[pl.ds(2 * j, 2), i * OWN:(i + 1) * OWN, :].reshape(2 * OWN, WID)
            if first:
                proj[i] = dot(t, chunk)
            else:
                proj[i] += dot(t, chunk)

    gather_w.step_across()
    gather_w.sib_own()
    project(p.z, p.x, True)
    gather_w.step_sides()
    loads[1].wait()
    gather_o.start()
    gather_w.sib_across()
    project(1 - p.z, p.x)
    gather_w.step_sides_across()
    gather_w.sib_sides()
    project(p.z, p.xl)
    project(p.z, p.xr)
    gather_w.step_opposite()
    gather_o.step_across()
    gather_w.sib_sides_across()
    project(1 - p.z, p.xl)
    project(1 - p.z, p.xr)
    gather_w.sib_opposite()
    project(p.z, p.xo)
    gather_w.step_last()
    gather_o.step_sides()
    gather_w.sib_last()
    project(1 - p.z, p.xo)

    def scale_of(raw):
        return lax.rsqrt(jnp.mean(raw * raw, axis=-1, keepdims=True) + EPS)

    for h in range(NH):
        hs = slice(h * HD, (h + 1) * HD)
        raw = proj[1, :, hs]
        kv[p.me, :, hs] = (raw * scale_of(raw)).astype(BF)
    kv[p.me, :, WID:] = proj[2].astype(BF)
    gather_kv.start()
    for h in range(NH):
        hs = slice(h * HD, (h + 1) * HD)
        raw = proj[0, :, hs]
        unit = (raw * scale_of(raw)).astype(BF)
        q[:, hs] = unit
        qt[h] = unit.T

    def forward(t, m, i, first=False):
        for h in range(NH):
            hs = slice(h * HD, (h + 1) * HD)
            vs = slice(WID + h * HD, WID + (h + 1) * HD)
            scores = dot_nt(q[:, hs], kv[t, :, hs])
            we = jnp.exp2(scores * EXP2_SCALE) * mask[m]
            wexp[i, h] = we
            part = we[:, :HD] + we[:, HD:]
            val = dot(we.astype(BF), kv[t, :, vs])
            if first:
                den[h] = part
                num[:, hs] = val
            else:
                den[h] += part
                num[:, hs] += val

    def loop2(fn):
        lax.fori_loop(0, 2, lambda i, carry: (fn(i), carry)[1], 0)

    gather_o.step_sides_across()
    forward(p.me, 0, 0, True)
    gather_kv.step_across()
    gather_kv.sib_own()
    forward(p.sib, 1, 2)
    gather_o.step_opposite()
    gather_kv.step_sides()
    forward(p.across, 0, 1)
    gather_o.step_last()
    gather_kv.sib_across()
    forward(at_tile(1 - p.z, p.x, 1 - p.c), 1, 3)
    gather_kv.step_sides_across()
    gather_o.sib_own()
    gather_o.sib_across()
    gather_o.sib_sides()
    gather_o.sib_sides_across()
    gather_o.sib_opposite()
    gather_o.sib_last()

    def grad_att(j, acc):
        cols = pl.ds(pl.multiple_of(j * 384, 384), 384)
        return acc + dot(cot[:, cols], wo[pl.ds(2 * j, 2)].reshape(2 * OWN, WID))

    g[...] = lax.fori_loop(0, 8, grad_att, jnp.zeros((ROWS, WID), F32)).astype(BF)
    for h in range(NH):
        gt[h] = g[:, h * HD:(h + 1) * HD].T
    def side(zz, i):
        forward(at_tile(zz, p.xl, 1 - p.c), 2, 4 + 2 * i)
        forward(at_tile(zz, p.xr, 1 - p.c), 2, 5 + 2 * i)

    gather_kv.sib_sides()
    side(p.z, 0)
    gather_kv.step_opposite()
    forward(at_tile(p.z, p.xo, p.c), 0, 8)
    gather_kv.sib_sides_across()
    side(1 - p.z, 1)
    gather_kv.step_last()
    gather_kv.sib_opposite()
    forward(at_tile(p.z, p.xo, 1 - p.c), 1, 10)
    forward(at_tile(1 - p.z, p.xo, p.c), 0, 9)
    gather_kv.sib_last()
    forward(at_tile(1 - p.z, p.xo, 1 - p.c), 1, 11)

    for h in range(NH):
        hs = slice(h * HD, (h + 1) * HD)
        inverse = 1.0 / jnp.sum(den[h], axis=-1, keepdims=True)
        context = num[:, hs] * inverse
        att[0, :, hs] = context.astype(BF)
        row = jnp.sum(g[:, hs].astype(F32) * context, axis=-1, keepdims=True)
        delta[h] = jnp.broadcast_to(row, (ROWS, HD))
        den[h] = jnp.broadcast_to(inverse, (ROWS, HD))
    att_swap = to_sibling(2, att.at[0], att.at[1])

    def backward(t, i, dst, first=False, adding=False):
        for h in range(NH):
            hs = slice(h * HD, (h + 1) * HD)
            vs = slice(WID + h * HD, WID + (h + 1) * HD)
            grad = dot_nt(g[:, hs], kv[t, :, vs])
            inverse, row = den[h], delta[h]
            probs, ds = [], []
            for part in range(2):
                cs = slice(part * HD, (part + 1) * HD)
                pr = wexp[i, h, :, cs] * inverse
                ds.append((pr * (grad[:, cs] - row)).astype(BF))
                probs.append(pr.astype(BF))
            probs = jnp.concatenate(probs, axis=1)
            ds = jnp.concatenate(ds, axis=1)
            term = dot(ds, kv[t, :, hs])
            if first:
                dq[:, hs] = term
            else:
                dq[:, hs] += term
            dk = dot(qt[h], ds) * INV_ROOT
            dv = dot(gt[h], probs)
            if adding:
                dk = dk + dst[hs].astype(F32)
                dv = dv + dst[vs].astype(F32)
            dst[hs] = dk.astype(BF)
            dst[vs] = dv.astype(BF)

    def swap_copy(x, z, k):
        return pltpu.make_async_remote_copy(
            src_ref=dkv_out.at[x, z], dst_ref=dkv_parts.at[x, z], send_sem=dkv_send.at[k],
            recv_sem=dkv_recv.at[k], device_id={"tile": p.sib}, device_id_type=MESH)

    def swap(x, z, k):
        c = swap_copy(x, z, k)
        c.start()
        sent.append(c)

    def out_part(j, carry):
        hd_parts[j // 2, j % 2] = dot_nt(att[0], wo[pl.ds(2 * j, 2)].reshape(2 * OWN, WID)).astype(BF)
        return carry

    def opposite_sib(i):
        zz = (p.z + i) % 2
        backward(at_tile(zz, p.xo, 1 - p.c), 10 + i, dkv_out.at[p.xo, zz])

    def out_grad(j, carry):
        go_parts[j % 4, j // 4] = (dot(cot_t[j, p.c], att[0]) + dot(cot_sib[j], att[1])).astype(BF)
        return carry

    cot_swap.wait_recv()
    att_swap.wait_recv()
    lax.fori_loop(0, 8, out_grad, 0)
    sum_go.start_far()
    sum_go.start_near()
    sum_go.start_own()

    dq[...] = jnp.zeros_like(dq)
    loop2(opposite_sib)
    swap(p.xo, p.z, 0)
    swap(p.xo, 1 - p.z, 1)
    lax.fori_loop(0, 8, out_part, 0)
    sum_out.start_far()
    sum_out.start_near()
    for i, zz in enumerate((p.z, 1 - p.z)):
        swap_copy(p.xo, zz, i).wait_recv()

    def opposite_own(i):
        zz = (p.z + i) % 2
        backward(at_tile(zz, p.xo, p.c), 8 + i, dkv_parts.at[p.xo, zz], adding=True)

    loop2(opposite_own)
    sum_dkv.start_far()
    sum_go.step_far_b()
    sum_go.step_near()

    def sides_sib(i):
        zz = (p.z + i) % 2
        backward(at_tile(zz, p.xl, 1 - p.c), 4 + 2 * i, dkv_out.at[p.xl, zz])
        backward(at_tile(zz, p.xr, 1 - p.c), 5 + 2 * i, dkv_out.at[p.xr, zz])

    loop2(sides_sib)
    for i, zz in enumerate((p.z, 1 - p.z)):
        swap(p.xl, zz, 2 + i)
        swap(p.xr, zz, 4 + i)
    sum_dkv.step_far_b()
    sum_go.step_near_b()
    for i, zz in enumerate((p.z, 1 - p.z)):
        swap_copy(p.xl, zz, 2 + i).wait_recv()
        swap_copy(p.xr, zz, 4 + i).wait_recv()
    sum_dkv.start_near()
    sum_out.step_near()

    def own_sib(i):
        zz = (p.z + i) % 2
        backward(at_tile(zz, p.x, 1 - p.c), 2 + i, dkv_out.at[p.x, zz])

    loop2(own_sib)
    for i, zz in enumerate((p.z, 1 - p.z)):
        swap(p.x, zz, 6 + i)
    sum_dkv.step_near()
    sum_dkv.step_near_b()
    for i, zz in enumerate((p.z, 1 - p.z)):
        swap_copy(p.x, zz, 6 + i).wait_recv()

    def own_own(i):
        zz = (p.z + i) % 2
        backward(at_tile(zz, p.x, p.c), i, dkv_parts.at[p.x, zz], adding=True)

    loop2(own_own)
    sum_dkv.start_own()

    def unit_back(grad, raw):
        scale = scale_of(raw)
        unit = raw * scale
        return scale * (grad - unit * jnp.mean(grad * unit, axis=-1, keepdims=True))

    for h in range(NH):
        hs = slice(h * HD, (h + 1) * HD)
        gp[0, 0, :, hs] = unit_back(dq[:, hs] * INV_ROOT, proj[0, :, hs]).astype(BF)
    sum_go.step_pair()
    sum_dkv.step_pair()
    sum_out.step_pair()
    sum_dkv.result(dkv_sum)
    for h in range(NH):
        hs = slice(h * HD, (h + 1) * HD)
        vs = slice(WID + h * HD, WID + (h + 1) * HD)
        gp[0, 1, :, hs] = unit_back(dkv_sum[hs].T, proj[1, :, hs]).astype(BF)
        gp[0, 2, :, hs] = dkv_sum[vs].T.astype(BF)
    gp_swap = to_sibling(3, gp.at[0], gp.at[1])

    tok_swap.wait_recv()
    gp_swap.wait_recv()

    def qkv_grad(j):
        for i in range(3):
            gq_parts[j % 4, j // 4, i * OWN:(i + 1) * OWN] = (
                dot(tok_t[j, p.c], gp[0, i]) + dot(tok_sib[j], gp[1, i])).astype(BF)

    loop2(lambda i: qkv_grad(i * 4 + p.xo))
    sum_gq.start_far()
    loop2(lambda i: qkv_grad(i * 4 + p.xr))
    loop2(lambda i: qkv_grad(i * 4 + p.xl))
    sum_gq.start_near()
    loop2(lambda i: qkv_grad(i * 4 + p.x))
    sum_gq.start_own()
    sum_out.result(out_ref)
    sum_out.finish()

    def tok_part(j, carry):
        acc = dot_nt(gp[0, 0], w[pl.ds(2 * j, 2), 0:OWN, :].reshape(2 * OWN, WID))
        for i in range(1, 3):
            acc += dot_nt(gp[0, i], w[pl.ds(2 * j, 2), i * OWN:(i + 1) * OWN, :].reshape(2 * OWN, WID))
        hd_parts[j // 2, j % 2] = acc.astype(BF)
        return carry

    lax.fori_loop(0, 8, tok_part, 0)
    sum_tok.start_far()
    sum_tok.start_near()
    sum_gq.step_far_b()
    sum_gq.step_near()
    sum_gq.step_near_b()
    sum_tok.step_near()
    sum_go.result(gout_ref)
    sum_gq.step_pair()
    sum_tok.step_pair()
    sum_gq.result(gqkv_ref)
    sum_tok.result(gtok_ref)

    for s in (gather_w, gather_o, gather_kv, sum_dkv, sum_gq, sum_go, sum_tok):
        s.finish()
    for c in sent:
        c.wait_send()


def lane_bufs(rows, first, cols):
    _, ah, _, bh = split_rows(rows, first)
    second = rows - first
    bufs = [(2, 2, ah[0].size, cols), (2, 2, first, cols), (first, cols)]
    if second:
        bufs += [(4, second, cols), (2, bh[1].size, cols), (2, second, cols)]
    return [pltpu.VMEM(b, BF) for b in bufs]


def deliver(*refs):
    for i in range(4):
        refs[4 + i][...] = refs[i][...]


def local(tokens, cotangent, qkv_weight, out_weight, slab_of_device, extents):
    w = jnp.transpose(qkv_weight, (1, 0, 2)).reshape(3 * OWN, WID)
    vm = lambda *shape, dtype=BF: pltpu.VMEM(shape, dtype)
    dma = lambda *shape: pltpu.SemaphoreType.DMA(shape)
    scratch = [
        vm(16, 3 * OWN, WID), vm(16, OWN, WID), vm(16, ROWS, 2 * WID), vm(ROWS, D), vm(ROWS, D),
        vm(8, 2, OWN, ROWS), vm(8, OWN, ROWS), vm(8, 2, OWN, ROWS), vm(8, OWN, ROWS),
        vm(12, NH, ROWS, ROWS, dtype=F32), vm(3, ROWS, ROWS, dtype=F32),
        vm(3, ROWS, WID, dtype=F32), vm(ROWS, WID), vm(NH, HD, ROWS), vm(ROWS, WID), vm(NH, HD, ROWS),
        vm(ROWS, WID, dtype=F32), vm(NH, ROWS, HD, dtype=F32), vm(NH, ROWS, HD, dtype=F32),
        vm(ROWS, WID, dtype=F32), vm(2, ROWS, WID), vm(2, 3, ROWS, WID), vm(2 * WID, ROWS, dtype=F32),
        vm(4, 2, 2 * WID, ROWS), vm(4, 2, 2 * WID, ROWS), *lane_bufs(2 * WID, DKV_FIRST, ROWS),
        vm(4, 2, 3 * OWN, WID), *lane_bufs(3 * OWN, QKV_FIRST, WID),
        vm(4, 2, OWN, WID), *lane_bufs(OWN, OUT_FIRST, WID),
        vm(4, 2, ROWS, WID), *lane_bufs(ROWS, ROWS, WID), *lane_bufs(ROWS, ROWS, WID),
        dma(4), dma(3, GATHER_COPIES), dma(3, GATHER_COPIES), dma(5, SCATTER_COPIES), dma(5, SCATTER_COPIES),
        dma(4), dma(4), dma(8), dma(8),
    ]
    any_spec = pl.BlockSpec(memory_space=pl.ANY)
    smem = pl.BlockSpec(memory_space=pltpu.SMEM)
    vmem = pl.BlockSpec(memory_space=pltpu.VMEM)
    shapes = (
        jax.ShapeDtypeStruct((ROWS, WID), BF), jax.ShapeDtypeStruct((ROWS, WID), BF),
        jax.ShapeDtypeStruct((3 * OWN, WID), F32), jax.ShapeDtypeStruct((OWN, WID), F32))
    results = pl.pallas_call(
        kernel,
        out_shape=shapes,
        in_specs=[any_spec] * 4 + [smem] * 2,
        out_specs=(vmem,) * 4,
        scratch_shapes=scratch,
        compiler_params=pltpu.CompilerParams(
            collective_id=0, has_side_effects=True, vmem_limit_bytes=64 * 1024 * 1024),
        cost_estimate=pl.CostEstimate(flops=20_000_000_000, bytes_accessed=10_000_000, transcendentals=2_400_000),
        name="sublayer",
    )(tokens, cotangent, w, out_weight, slab_of_device, extents.T)
    output, grad_tokens, grad_qkv, grad_out = pl.pallas_call(
        deliver, out_shape=shapes, in_specs=[vmem] * 4, out_specs=(vmem,) * 4, name="deliver")(*results)
    grad_qkv = jnp.transpose(grad_qkv.reshape(3, OWN, WID), (1, 0, 2))
    return output, grad_tokens, grad_qkv, grad_out


def solution(mesh):
    return jax.shard_map(
        local, mesh=mesh,
        in_specs=(P("tile", None), P("tile", None), P("tile", None, "head"), P("tile", "head"), P(None), P(None, None)),
        out_specs=(P("tile", "head"), P("tile", "head"), P("tile", None, "head"), P("tile", "head")),
        check_vma=False)
```

time: 180 us -> 148 us (0.82)
  Pallas kernels: 171 us -> 147 us
  local copies, waits for them, and re-layouts: 7.5 us -> 0 us
    pallas_call x1 -> x2, Pallas kernels: 171 us -> 147 us  [the longest x1 144 us: local(): pl.pallas_call(kernel, out_shape=shapes, in_specs=[any_spec] * 4 + [smem]...]
    unnamed x7 -> x0, local copies, waits for them, and re-layouts: 7.5 us -> none
where the time goes in v2:
time: 148 us
  Pallas kernels  147 us (99%)
    pallas_call x1, Pallas kernels, local(): pl.pallas_call(kernel, out_shape=shapes, in_specs=[any_spec] * 4 + [smem]...  144 us

profile of v2, /device:TPU:1, one launch (start us, length us, event | category | flops | bytes accessed | tf_op | source)
XLA Modules:
  0.0 147.6 jit_solution(5834978356786400762)
XLA Ops:
  0.6 144.4 %sublayer.1 = (bf16[256,384]{1,0:T(8,128)(2,1)}, bf16[256,384]{1,0:T(8,128)(2,1)}, f32[576,384]{1,0:T(8,128)}, f32[192,384]{1,0:T(8,128)}) custom-call(bf16[256,3072]{1,0:T(8,128)(2,1)} %tok_hbm.1, bf16[256,3072]{1,0:T(8,128)(2,1)} %cot_hbm.1, bf16[576,384]{1,0:T(8,128)(2,1)} %bitcast.8, bf16[192,384]{1,0:T(8,128)(2,1)} %wo_hbm.1, s32[16]{0:T(128)} %slab.1, ...), custom_call_target="tpu_custom_call" | custom-call | flops 20000000000 | bytes 10000000 | tf_op jit(solution)/shard_map/sublayer/pallas_call | solution.py:715
  145.0 2.6 %deliver.1 = (bf16[256,384]{1,0:T(8,128)(2,1)}, bf16[256,384]{1,0:T(8,128)(2,1)}, f32[576,384]{1,0:T(8,128)}, f32[192,384]{1,0:T(8,128)}) custom-call(bf16[256,384]{1,0:T(8,128)(2,1)} %get-tuple-element.12.refs_0_, bf16[256,384]{1,0:T(8,128)(2,1)} %get-tuple-element.13.refs_1_, f32[576,384]{1,0:T(8,128)} %get-tuple-element.14.refs_2_, ...), custom_call_target="tpu_custom_call" | custom-call | tf_op jit(solution)/shard_map/deliver/pallas_call | solution.py:726

commit v3 on v2

--- a/solution.py
+++ b/solution.py
@@ -20,8 +20,9 @@
 BF = jnp.bfloat16
 F32 = jnp.float32
 GATHER_COPIES = 32
-SCATTER_COPIES = 17
-QKV_FIRST, OUT_FIRST, KV_FIRST, DKV_FIRST = 320, 112, 144, 432
+SCATTER_COPIES = 23
+SUM_FIRST = 128
+QKV_FIRST, OUT_FIRST, KV_FIRST, DKV_FIRST, KVW_FIRST = 320, 112, 144, 496, 256
 
 
 def dot(a, b):
@@ -81,12 +82,21 @@
         self.go(0, p.me, self.a, p.across)
         self.go(1, p.me, self.b, p.right)
         self.go(2, p.me, self.b, p.left)
-        self.go(3, p.me, self.a, p.right)
-        self.go(4, p.me, self.a, p.left)
-        self.go(5, p.me, self.b, p.across)
         c = self.copy(6, self.buf.at[p.me], p.sib)
         c.start()
         self.sent.append(c)
+
+    def start_rest(self, in_turn):
+        p = self.p
+        if in_turn:
+            for c in self.sent[1:3]:
+                c.wait_send()
+        self.go(3, p.me, self.a, p.right)
+        self.go(4, p.me, self.a, p.left)
+        if in_turn:
+            self.sent[0].wait_send()
+            del self.sent[:3]
+        self.go(5, p.me, self.b, p.across)
 
     def step_across(self):
         p = self.p
@@ -111,26 +121,27 @@
         self.go(17, p.right, self.b, p.sib)
         self.go(18, p.left, self.a, p.sib)
         self.go(19, p.right, self.a, p.sib)
-        self.got(5, p.across, self.b)
-        self.go(20, p.across, self.b, p.sib)
 
     def step_sides_across(self):
         p = self.p
         zl, zr = at_tile(1 - p.z, p.xl, p.c), at_tile(1 - p.z, p.xr, p.c)
+        to = at_tile(p.z, p.xo, p.c)
+        self.got(10, to, self.bh[0])
+        self.got(12, to, self.bh[1])
+        self.go(25, to, self.b, p.across)
         self.got(7, zl, self.a)
         self.go(21, zl, self.ah[0], p.right)
         self.got(8, zr, self.a)
         self.go(22, zr, self.ah[1], p.left)
         self.go(23, zl, self.a, p.sib)
         self.go(24, zr, self.a, p.sib)
+        self.got(5, p.across, self.b)
+        self.go(20, p.across, self.b, p.sib)
 
     def step_opposite(self):
         p = self.p
         zl, zr = at_tile(1 - p.z, p.xl, p.c), at_tile(1 - p.z, p.xr, p.c)
         to = at_tile(p.z, p.xo, p.c)
-        self.got(10, to, self.bh[0])
-        self.got(12, to, self.bh[1])
-        self.go(25, to, self.b, p.across)
         self.got(14, to, self.ah[0])
         self.got(15, to, self.ah[1])
         c = self.copy(26, self.buf.at[to], p.sib)
@@ -221,77 +232,94 @@
         self.parts[ring, pair, rows] = (
             self.parts[ring, pair, rows].astype(F32) + got.astype(F32)).astype(BF)
 
+
+    def pairs(self):
+        return (0, 1 - self.pair), (1, self.pair)
+
     def start_z(self, k, ring):
-        self.go(k, self.parts.at[ring, 1 - self.pair, self.b], self.zed.at[ring], self.across)
+        if self.zed is not None:
+            self.go(k, self.parts.at[ring, 1 - self.pair, self.b], self.zed.at[ring], self.across)
 
     def got_z(self, k, ring):
         self.got(k, self.zed.at[ring])
 
-    def start_far(self):
-        if self.zed is not None:
+    def far_at(self, i, n):
+        return self.far.at[i, n, pl.ds(0, self.ah[i].size)]
+
+    def start_far(self, n, over=True):
+        z = self.pairs()[n][1]
+        for i, dev in enumerate((self.right, self.left)):
+            self.go(4 + 2 * n + i, self.parts.at[self.ro, z, self.ah[i]], self.far_at(i, n), dev)
+        if n == 0 and over:
             self.start_z(0, self.ro)
-        for i, dev in enumerate((self.right, self.left)):
-            self.go(4 + i, self.parts.at[self.ro, :, self.ah[i]], self.far.at[i, :, pl.ds(0, self.ah[i].size)], dev)
-
-    def start_near(self):
-        if self.zed is not None:
-            self.start_z(1, self.rr)
-            self.start_z(2, self.rl)
-        self.go(6, self.parts.at[self.rr, :, self.ah[1]], self.near.at[0, :, self.ah[1]], self.right)
-        self.go(7, self.parts.at[self.rl, :, self.ah[0]], self.near.at[1, :, self.ah[0]], self.left)
+
+    def start_near(self, n, over=True):
+        z = self.pairs()[n][1]
+        for i, (ring, dev) in enumerate(((self.rr, self.right), (self.rl, self.left))):
+            rows = self.ah[1 - i]
+            self.go(8 + 2 * n + i, self.parts.at[ring, z, rows], self.near.at[i, n, rows], dev)
+            if n == 0 and over:
+                self.start_z(1 + i, ring)
 
     def start_own(self):
         self.start_z(3, self.ring)
+
+    def start_over(self):
+        for k, ring in enumerate((self.ro, self.rr, self.rl, self.ring)):
+            self.start_z(k, ring)
 
     def step_far_b(self):
         self.got_z(0, self.ro)
         self.add(self.ro, self.pair, self.b, self.zed[self.ro])
         for i, dev in enumerate((self.right, self.left)):
-            self.go(10 + i, self.parts.at[self.ro, self.pair, self.bh[i]], self.far_b.at[i, pl.ds(0, self.bh[i].size)], dev)
-
-    def step_near(self):
+            self.go(16 + i, self.parts.at[self.ro, self.pair, self.bh[i]], self.far_b.at[i, pl.ds(0, self.bh[i].size)], dev)
+
+    def step_near(self, n):
+        z = self.pairs()[n][1]
         for i, (ring, dev) in enumerate(((self.rr, self.right), (self.rl, self.left))):
-            got = self.far.at[i, :, pl.ds(0, self.ah[i].size)]
-            self.got(4 + i, got)
-            for z in range(2):
-                self.add(ring, z, self.ah[i], got[z])
-            self.go(8 + i, self.parts.at[ring, :, self.ah[i]], self.near.at[i, :, self.ah[i]], dev)
+            rows, got = self.ah[i], self.far_at(i, n)
+            self.got(4 + 2 * n + i, got)
+            self.add(ring, z, rows, got[...])
+            self.go(12 + 2 * n + i, self.parts.at[ring, z, rows], self.near.at[i, n, rows], dev)
 
     def step_near_b(self):
         for i, (ring, dev) in enumerate(((self.rr, self.right), (self.rl, self.left))):
             self.got_z(1 + i, ring)
             self.add(ring, self.pair, self.b, self.zed[ring])
             j = 1 - i
-            self.go(12 + i, self.parts.at[ring, self.pair, self.bh[j]], self.near_b.at[i, self.bl[j]], dev)
+            self.go(18 + i, self.parts.at[ring, self.pair, self.bh[j]], self.near_b.at[i, self.bl[j]], dev)
         for i, (ring, dev) in enumerate(((self.rr, self.right), (self.rl, self.left))):
             got = self.far_b.at[i, pl.ds(0, self.bh[i].size)]
-            self.got(10 + i, got)
+            self.got(16 + i, got)
             self.add(ring, self.pair, self.bh[i], got[...])
-            self.go(14 + i, self.parts.at[ring, self.pair, self.bh[i]], self.near_b.at[i, self.bl[i]], dev)
-
-    def total(self, pair):
-        return (self.parts[self.ring, pair, self.a].astype(F32) + self.near[0, pair].astype(F32)
-                + self.near[1, pair].astype(F32))
+            self.go(20 + i, self.parts.at[ring, self.pair, self.bh[i]], self.near_b.at[i, self.bl[i]], dev)
+
+    def total(self, n):
+        for i in range(2):
+            self.got(8 + 2 * n + i, self.near.at[i, n, self.ah[1 - i]])
+            self.got(12 + 2 * n + i, self.near.at[i, n, self.ah[i]])
+        z = self.pairs()[n][1]
+        return (self.parts[self.ring, z, self.a].astype(F32) + self.near[0, n].astype(F32)
+                + self.near[1, n].astype(F32))
 
     def step_pair(self):
+        other = 1 - self.pair
+        self.parts[self.ring, other, self.a] = self.total(0).astype(BF)
+        self.go(22, self.parts.at[self.ring, other, self.a], self.last, self.across)
+
+    def result_b(self, out):
+        self.got_z(3, self.ring)
         for i in range(2):
-            self.got(6 + i, self.near.at[i, :, self.ah[1 - i]])
-            self.got(8 + i, self.near.at[i, :, self.ah[i]])
-        other = 1 - self.pair
-        self.parts[self.ring, other, self.a] = self.total(other).astype(BF)
-        self.go(16, self.parts.at[self.ring, other, self.a], self.last, self.across)
-
-    def result(self, out):
-        if self.zed is not None:
-            self.got_z(3, self.ring)
-            for i in range(2):
-                self.got(12 + i, self.near_b.at[i, self.bl[1 - i]])
-                self.got(14 + i, self.near_b.at[i, self.bl[i]])
-            out[self.b] = (
-                (self.parts[self.ring, self.pair, self.b].astype(F32) + self.zed[self.ring].astype(F32))
-                + (self.near_b[0].astype(F32) + self.near_b[1].astype(F32))).astype(out.dtype)
-        self.got(16, self.last)
-        out[self.a] = (self.total(self.pair) + self.last[...].astype(F32)).astype(out.dtype)
+            self.got(18 + i, self.near_b.at[i, self.bl[1 - i]])
+            self.got(20 + i, self.near_b.at[i, self.bl[i]])
+        out[self.b] = (
+            (self.parts[self.ring, self.pair, self.b].astype(F32) + self.zed[self.ring].astype(F32))
+            + (self.near_b[0].astype(F32) + self.near_b[1].astype(F32))).astype(out.dtype)
+
+    def result_a(self, out):
+        own = self.total(1)
+        self.got(22, self.last)
+        out[self.a] = (own + self.last[...].astype(F32)).astype(out.dtype)
 
     def finish(self):
         for c in self.sent:
@@ -304,8 +332,9 @@
            proj, q, qt, g, gt, num, den, delta, dq, att, gp, dkv_sum,
            dkv_out, dkv_parts, dkv_far, dkv_near, dkv_last, dkv_zed, dkv_far_b, dkv_near_b,
            gq_parts, gq_far, gq_near, gq_last, gq_zed, gq_far_b, gq_near_b,
+           gk_parts, gk_far, gk_near, gk_last, gk_zed, gk_far_b, gk_near_b,
            go_parts, go_far, go_near, go_last, go_zed, go_far_b, go_near_b,
-           hd_parts, ho_far, ho_near, ho_last, ht_far, ht_near, ht_last,
+           ho_parts, ho_far, ho_near, ho_last, ht_parts, ht_far, ht_near, ht_last,
            load_sem, gat_send, gat_recv, sca_send, sca_recv, sib_send, sib_recv, dkv_send, dkv_recv):
     p = Place()
     hd = lax.axis_index("head")
@@ -343,10 +372,11 @@
     head_scatter = lambda i, parts, *bufs: Scatter(
         "head", hy, hz, head_devices, parts, ROWS, bufs, sca_send.at[i], sca_recv.at[i])
     sum_dkv = scatter(0, dkv_parts, DKV_FIRST, dkv_far, dkv_near, dkv_last, dkv_zed, dkv_far_b, dkv_near_b)
-    sum_gq = scatter(1, gq_parts, QKV_FIRST, gq_far, gq_near, gq_last, gq_zed, gq_far_b, gq_near_b)
-    sum_go = scatter(2, go_parts, OUT_FIRST, go_far, go_near, go_last, go_zed, go_far_b, go_near_b)
-    sum_out = head_scatter(3, hd_parts, ho_far, ho_near, ho_last)
-    sum_tok = head_scatter(4, hd_parts, ht_far, ht_near, ht_last)
+    sum_gk = scatter(5, gk_parts, KVW_FIRST, gk_far, gk_near, gk_last, gk_zed, gk_far_b, gk_near_b)
+    sum_gq = scatter(1, gq_parts, SUM_FIRST, gq_far, gq_near, gq_last, gq_zed, gq_far_b, gq_near_b)
+    sum_go = scatter(2, go_parts, SUM_FIRST, go_far, go_near, go_last, go_zed, go_far_b, go_near_b)
+    sum_out = head_scatter(3, ho_parts, ho_far, ho_near, ho_last)
+    sum_tok = head_scatter(4, ht_parts, ht_far, ht_near, ht_last)
 
     loads[0].wait()
     gather_w.start()
@@ -388,27 +418,30 @@
             else:
                 proj[i] += dot(t, chunk)
 
+    gather_w.start_rest(True)
     gather_w.step_across()
     gather_w.sib_own()
     project(p.z, p.x, True)
     gather_w.step_sides()
     loads[1].wait()
     gather_o.start()
-    gather_w.sib_across()
-    project(1 - p.z, p.x)
-    gather_w.step_sides_across()
+    gather_o.start_rest(False)
     gather_w.sib_sides()
     project(p.z, p.xl)
     project(p.z, p.xr)
+    gather_w.step_sides_across()
+    gather_o.step_across()
+    gather_w.sib_across()
+    project(1 - p.z, p.x)
     gather_w.step_opposite()
-    gather_o.step_across()
+    gather_o.step_sides()
     gather_w.sib_sides_across()
     project(1 - p.z, p.xl)
     project(1 - p.z, p.xr)
     gather_w.sib_opposite()
     project(p.z, p.xo)
     gather_w.step_last()
-    gather_o.step_sides()
+    gather_o.step_sides_across()
     gather_w.sib_last()
     project(1 - p.z, p.xo)
 
@@ -447,42 +480,41 @@
     def loop2(fn):
         lax.fori_loop(0, 2, lambda i, carry: (fn(i), carry)[1], 0)
 
-    gather_o.step_sides_across()
+    def grad_att(j, acc):
+        cols = pl.ds(pl.multiple_of(j * 384, 384), 384)
+        return acc + dot(cot[:, cols], wo[pl.ds(2 * j, 2)].reshape(2 * OWN, WID))
+
+    def side(zz, i):
+        forward(at_tile(zz, p.xl, 1 - p.c), 2, 4 + 2 * i)
+        forward(at_tile(zz, p.xr, 1 - p.c), 2, 5 + 2 * i)
+
     forward(p.me, 0, 0, True)
+    gather_kv.start_rest(True)
     gather_kv.step_across()
     gather_kv.sib_own()
+    gather_o.step_opposite()
     forward(p.sib, 1, 2)
-    gather_o.step_opposite()
     gather_kv.step_sides()
+    gather_kv.step_sides_across()
     forward(p.across, 0, 1)
+    gather_kv.sib_sides()
+    side(p.z, 0)
     gather_o.step_last()
     gather_kv.sib_across()
     forward(at_tile(1 - p.z, p.x, 1 - p.c), 1, 3)
-    gather_kv.step_sides_across()
+    gather_kv.step_opposite()
+    forward(at_tile(p.z, p.xo, p.c), 0, 8)
+    gather_kv.sib_sides_across()
+    side(1 - p.z, 1)
     gather_o.sib_own()
     gather_o.sib_across()
     gather_o.sib_sides()
     gather_o.sib_sides_across()
     gather_o.sib_opposite()
     gather_o.sib_last()
-
-    def grad_att(j, acc):
-        cols = pl.ds(pl.multiple_of(j * 384, 384), 384)
-        return acc + dot(cot[:, cols], wo[pl.ds(2 * j, 2)].reshape(2 * OWN, WID))
-
     g[...] = lax.fori_loop(0, 8, grad_att, jnp.zeros((ROWS, WID), F32)).astype(BF)
     for h in range(NH):
         gt[h] = g[:, h * HD:(h + 1) * HD].T
-    def side(zz, i):
-        forward(at_tile(zz, p.xl, 1 - p.c), 2, 4 + 2 * i)
-        forward(at_tile(zz, p.xr, 1 - p.c), 2, 5 + 2 * i)
-
-    gather_kv.sib_sides()
-    side(p.z, 0)
-    gather_kv.step_opposite()
-    forward(at_tile(p.z, p.xo, p.c), 0, 8)
-    gather_kv.sib_sides_across()
-    side(1 - p.z, 1)
     gather_kv.step_last()
     gather_kv.sib_opposite()
     forward(at_tile(p.z, p.xo, 1 - p.c), 1, 10)
@@ -537,138 +569,184 @@
         c.start()
         sent.append(c)
 
-    def out_part(j, carry):
-        hd_parts[j // 2, j % 2] = dot_nt(att[0], wo[pl.ds(2 * j, 2)].reshape(2 * OWN, WID)).astype(BF)
-        return carry
+    def out_part(ring):
+        def one(i):
+            o = wo[pl.ds(4 * ring + 2 * i, 2)].reshape(2 * OWN, WID)
+            ho_parts[ring, i] = dot_nt(att[0], o).astype(BF)
+        loop2(one)
+
+    def tok_part(ring):
+        def one(i):
+            j = 2 * ring + i
+            acc = dot_nt(gp[0, 0], w[pl.ds(2 * j, 2), 0:OWN, :].reshape(2 * OWN, WID))
+            for n in range(1, 3):
+                acc += dot_nt(gp[0, n], w[pl.ds(2 * j, 2), n * OWN:(n + 1) * OWN, :].reshape(2 * OWN, WID))
+            ht_parts[ring, i] = acc.astype(BF)
+        loop2(one)
+
+    def out_grad(ring):
+        def one(i):
+            j = 4 * i + ring
+            go_parts[ring, i] = (dot(cot_t[j, p.c], att[0]) + dot(cot_sib[j], att[1])).astype(BF)
+        loop2(one)
+
+    def qkv_grad(parts, j, which):
+        for n, i in enumerate(which):
+            parts[j % 4, j // 4, n * OWN:(n + 1) * OWN] = (
+                dot(tok_t[j, p.c], gp[0, i]) + dot(tok_sib[j], gp[1, i])).astype(BF)
+
+    def kv_grad(ring):
+        loop2(lambda i: qkv_grad(gk_parts, i * 4 + ring, (1, 2)))
 
     def opposite_sib(i):
         zz = (p.z + i) % 2
         backward(at_tile(zz, p.xo, 1 - p.c), 10 + i, dkv_out.at[p.xo, zz])
 
-    def out_grad(j, carry):
-        go_parts[j % 4, j // 4] = (dot(cot_t[j, p.c], att[0]) + dot(cot_sib[j], att[1])).astype(BF)
-        return carry
-
-    cot_swap.wait_recv()
-    att_swap.wait_recv()
-    lax.fori_loop(0, 8, out_grad, 0)
-    sum_go.start_far()
-    sum_go.start_near()
-    sum_go.start_own()
-
-    dq[...] = jnp.zeros_like(dq)
-    loop2(opposite_sib)
-    swap(p.xo, p.z, 0)
-    swap(p.xo, 1 - p.z, 1)
-    lax.fori_loop(0, 8, out_part, 0)
-    sum_out.start_far()
-    sum_out.start_near()
-    for i, zz in enumerate((p.z, 1 - p.z)):
-        swap_copy(p.xo, zz, i).wait_recv()
-
     def opposite_own(i):
-        zz = (p.z + i) % 2
-        backward(at_tile(zz, p.xo, p.c), 8 + i, dkv_parts.at[p.xo, zz], adding=True)
-
-    loop2(opposite_own)
-    sum_dkv.start_far()
-    sum_go.step_far_b()
-    sum_go.step_near()
+        zz = (p.z + 1 + i) % 2
+        backward(at_tile(zz, p.xo, p.c), 9 - i, dkv_parts.at[p.xo, zz], adding=True)
 
     def sides_sib(i):
-        zz = (p.z + i) % 2
-        backward(at_tile(zz, p.xl, 1 - p.c), 4 + 2 * i, dkv_out.at[p.xl, zz])
-        backward(at_tile(zz, p.xr, 1 - p.c), 5 + 2 * i, dkv_out.at[p.xr, zz])
-
-    loop2(sides_sib)
-    for i, zz in enumerate((p.z, 1 - p.z)):
-        swap(p.xl, zz, 2 + i)
-        swap(p.xr, zz, 4 + i)
-    sum_dkv.step_far_b()
-    sum_go.step_near_b()
-    for i, zz in enumerate((p.z, 1 - p.z)):
-        swap_copy(p.xl, zz, 2 + i).wait_recv()
-        swap_copy(p.xr, zz, 4 + i).wait_recv()
-    sum_dkv.start_near()
-    sum_out.step_near()
+        zz = (p.z + 1 + i) % 2
+        backward(at_tile(zz, p.xl, 1 - p.c), 6 - 2 * i, dkv_out.at[p.xl, zz])
+        backward(at_tile(zz, p.xr, 1 - p.c), 7 - 2 * i, dkv_out.at[p.xr, zz])
 
     def own_sib(i):
         zz = (p.z + i) % 2
         backward(at_tile(zz, p.x, 1 - p.c), 2 + i, dkv_out.at[p.x, zz])
 
-    loop2(own_sib)
-    for i, zz in enumerate((p.z, 1 - p.z)):
-        swap(p.x, zz, 6 + i)
-    sum_dkv.step_near()
-    sum_dkv.step_near_b()
-    for i, zz in enumerate((p.z, 1 - p.z)):
-        swap_copy(p.x, zz, 6 + i).wait_recv()
-
     def own_own(i):
         zz = (p.z + i) % 2
         backward(at_tile(zz, p.x, p.c), i, dkv_parts.at[p.x, zz], adding=True)
-
-    loop2(own_own)
-    sum_dkv.start_own()
 
     def unit_back(grad, raw):
         scale = scale_of(raw)
         unit = raw * scale
         return scale * (grad - unit * jnp.mean(grad * unit, axis=-1, keepdims=True))
 
+    dq[...] = jnp.zeros_like(dq)
+    loop2(opposite_sib)
+    swap(p.xo, 1 - p.z, 0)
+    swap(p.xo, p.z, 1)
+    cot_swap.wait_recv()
+    att_swap.wait_recv()
+    out_grad(p.xo)
+    sum_go.start_far(0, False)
+    sum_go.start_far(1, False)
+    out_grad(p.xr)
+    out_grad(p.xl)
+    sum_go.start_near(0, False)
+    sum_go.start_near(1, False)
+    swap_copy(p.xo, 1 - p.z, 0).wait_recv()
+    swap_copy(p.xo, p.z, 1).wait_recv()
+    loop2(opposite_own)
+    sum_dkv.start_far(0)
+    sum_dkv.start_far(1)
+    sides_sib(0)
+    swap(p.xl, 1 - p.z, 2)
+    swap(p.xr, 1 - p.z, 3)
+    sides_sib(1)
+    swap(p.xl, p.z, 4)
+    swap(p.xr, p.z, 5)
+    out_part(sum_out.ro)
+    sum_out.start_far(0)
+    sum_out.start_far(1)
+    swap_copy(p.xl, 1 - p.z, 2).wait_recv()
+    swap_copy(p.xr, 1 - p.z, 3).wait_recv()
+    sum_dkv.start_near(0)
+    out_part(sum_out.rr)
+    out_part(sum_out.rl)
+    sum_out.start_near(0)
+    sum_out.start_near(1)
+    swap_copy(p.xl, p.z, 4).wait_recv()
+    swap_copy(p.xr, p.z, 5).wait_recv()
+    sum_dkv.start_near(1)
+    loop2(own_sib)
+    swap(p.x, p.z, 6)
+    swap(p.x, 1 - p.z, 7)
+    sum_dkv.step_near(0)
+    sum_dkv.step_far_b()
+    sum_dkv.step_near(1)
+    sum_go.step_near(0)
+    sum_go.step_near(1)
+    swap_copy(p.x, p.z, 6).wait_recv()
+    swap_copy(p.x, 1 - p.z, 7).wait_recv()
+    loop2(own_own)
+    sum_dkv.start_own()
+    out_grad(p.x)
+    sum_go.start_over()
     for h in range(NH):
         hs = slice(h * HD, (h + 1) * HD)
         gp[0, 0, :, hs] = unit_back(dq[:, hs] * INV_ROOT, proj[0, :, hs]).astype(BF)
-    sum_go.step_pair()
+    gq_swap = to_sibling(3, gp.at[0, 0], gp.at[1, 0])
+    out_part(sum_out.ring)
+    sum_out.step_near(0)
+    sum_out.step_near(1)
+    sum_dkv.step_near_b()
+
+    tok_swap.wait_recv()
+    gq_swap.wait_recv()
+    lax.fori_loop(0, 8, lambda j, carry: (qkv_grad(gq_parts, j, (0,)), carry)[1], 0)
+    sum_gq.start_far(0, False)
+    sum_gq.start_far(1, False)
+    sum_gq.start_near(0, False)
+    sum_gq.start_near(1, False)
     sum_dkv.step_pair()
+    sum_dkv.result_b(dkv_sum)
     sum_out.step_pair()
-    sum_dkv.result(dkv_sum)
+    sum_dkv.result_a(dkv_sum)
+    sum_gq.start_over()
     for h in range(NH):
         hs = slice(h * HD, (h + 1) * HD)
         vs = slice(WID + h * HD, WID + (h + 1) * HD)
         gp[0, 1, :, hs] = unit_back(dkv_sum[hs].T, proj[1, :, hs]).astype(BF)
         gp[0, 2, :, hs] = dkv_sum[vs].T.astype(BF)
-    gp_swap = to_sibling(3, gp.at[0], gp.at[1])
-
-    tok_swap.wait_recv()
-    gp_swap.wait_recv()
-
-    def qkv_grad(j):
-        for i in range(3):
-            gq_parts[j % 4, j // 4, i * OWN:(i + 1) * OWN] = (
-                dot(tok_t[j, p.c], gp[0, i]) + dot(tok_sib[j], gp[1, i])).astype(BF)
-
-    loop2(lambda i: qkv_grad(i * 4 + p.xo))
-    sum_gq.start_far()
-    loop2(lambda i: qkv_grad(i * 4 + p.xr))
-    loop2(lambda i: qkv_grad(i * 4 + p.xl))
-    sum_gq.start_near()
-    loop2(lambda i: qkv_grad(i * 4 + p.x))
-    sum_gq.start_own()
-    sum_out.result(out_ref)
-    sum_out.finish()
-
-    def tok_part(j, carry):
-        acc = dot_nt(gp[0, 0], w[pl.ds(2 * j, 2), 0:OWN, :].reshape(2 * OWN, WID))
-        for i in range(1, 3):
-            acc += dot_nt(gp[0, i], w[pl.ds(2 * j, 2), i * OWN:(i + 1) * OWN, :].reshape(2 * OWN, WID))
-        hd_parts[j // 2, j % 2] = acc.astype(BF)
-        return carry
-
-    lax.fori_loop(0, 8, tok_part, 0)
-    sum_tok.start_far()
-    sum_tok.start_near()
+    gk_swap = to_sibling(4, gp.at[0, pl.ds(1, 2)], gp.at[1, pl.ds(1, 2)])
+
+    sum_go.step_far_b()
+    tok_part(sum_tok.ro)
+    sum_tok.start_far(0)
+    sum_tok.start_far(1)
+    gk_swap.wait_recv()
+    kv_grad(p.xo)
+    sum_gk.start_far(0)
+    sum_gk.start_far(1)
+    sum_go.step_pair()
+    sum_gq.step_near(0)
+    sum_gq.step_near(1)
+    sum_go.step_near_b()
+    tok_part(sum_tok.rr)
+    tok_part(sum_tok.rl)
+    sum_tok.start_near(0)
+    sum_tok.start_near(1)
+    kv_grad(p.xr)
+    kv_grad(p.xl)
+    sum_gk.start_near(0)
+    sum_gk.start_near(1)
     sum_gq.step_far_b()
-    sum_gq.step_near()
+    tok_part(sum_tok.ring)
+    sum_tok.step_near(0)
+    sum_tok.step_near(1)
+    kv_grad(p.x)
+    sum_gk.start_own()
+    sum_gk.step_near(0)
     sum_gq.step_near_b()
-    sum_tok.step_near()
-    sum_go.result(gout_ref)
+    sum_gk.step_far_b()
+    sum_gk.step_near(1)
+    sum_out.result_a(out_ref)
+    sum_go.result_b(gout_ref)
+    sum_go.result_a(gout_ref)
+    sum_tok.step_pair()
     sum_gq.step_pair()
-    sum_tok.step_pair()
-    sum_gq.result(gqkv_ref)
-    sum_tok.result(gtok_ref)
-
-    for s in (gather_w, gather_o, gather_kv, sum_dkv, sum_gq, sum_go, sum_tok):
+    sum_gk.step_near_b()
+    sum_gk.step_pair()
+    sum_gq.result_b(gqkv_ref.at[pl.ds(0, OWN)])
+    sum_gq.result_a(gqkv_ref.at[pl.ds(0, OWN)])
+    sum_tok.result_a(gtok_ref)
+    sum_gk.result_b(gqkv_ref.at[pl.ds(OWN, 2 * OWN)])
+    sum_gk.result_a(gqkv_ref.at[pl.ds(OWN, 2 * OWN)])
+
+    for s in (gather_w, gather_o, gather_kv, sum_dkv, sum_gq, sum_gk, sum_go, sum_out, sum_tok):
         s.finish()
     for c in sent:
         c.wait_send()
@@ -700,11 +778,12 @@
         vm(ROWS, WID, dtype=F32), vm(NH, ROWS, HD, dtype=F32), vm(NH, ROWS, HD, dtype=F32),
         vm(ROWS, WID, dtype=F32), vm(2, ROWS, WID), vm(2, 3, ROWS, WID), vm(2 * WID, ROWS, dtype=F32),
         vm(4, 2, 2 * WID, ROWS), vm(4, 2, 2 * WID, ROWS), *lane_bufs(2 * WID, DKV_FIRST, ROWS),
-        vm(4, 2, 3 * OWN, WID), *lane_bufs(3 * OWN, QKV_FIRST, WID),
-        vm(4, 2, OWN, WID), *lane_bufs(OWN, OUT_FIRST, WID),
-        vm(4, 2, ROWS, WID), *lane_bufs(ROWS, ROWS, WID), *lane_bufs(ROWS, ROWS, WID),
-        dma(4), dma(3, GATHER_COPIES), dma(3, GATHER_COPIES), dma(5, SCATTER_COPIES), dma(5, SCATTER_COPIES),
-        dma(4), dma(4), dma(8), dma(8),
+        vm(4, 2, OWN, WID), *lane_bufs(OWN, SUM_FIRST, WID),
+        vm(4, 2, 2 * OWN, WID), *lane_bufs(2 * OWN, KVW_FIRST, WID),
+        vm(4, 2, OWN, WID), *lane_bufs(OWN, SUM_FIRST, WID),
+        vm(4, 2, ROWS, WID), *lane_bufs(ROWS, ROWS, WID), vm(4, 2, ROWS, WID), *lane_bufs(ROWS, ROWS, WID),
+        dma(4), dma(3, GATHER_COPIES), dma(3, GATHER_COPIES), dma(6, SCATTER_COPIES), dma(6, SCATTER_COPIES),
+        dma(5), dma(5), dma(8), dma(8),
     ]
     any_spec = pl.BlockSpec(memory_space=pl.ANY)
     smem = pl.BlockSpec(memory_space=pltpu.SMEM)

time: 148 us -> 139 us (0.939)
  Pallas kernels: 147 us -> 138 us
    pallas_call x1, Pallas kernels: 144 us -> 136 us  [local(): pl.pallas_call(kernel, out_shape=shapes, in_specs=[any_spec] * 4 + [smem]...]
where the time goes in v3:
time: 139 us
  Pallas kernels  138 us (99%)
    pallas_call x1, Pallas kernels, local(): pl.pallas_call(kernel, out_shape=shapes, in_specs=[any_spec] * 4 + [smem]...  136 us

profile of v3, /device:TPU:1, one launch (start us, length us, event | category | flops | bytes accessed | tf_op | source)
XLA Modules:
  0.0 138.9 jit_solution(4673448858154002534)
XLA Ops:
  0.6 135.7 %sublayer.1 = (bf16[256,384]{1,0:T(8,128)(2,1)}, bf16[256,384]{1,0:T(8,128)(2,1)}, f32[576,384]{1,0:T(8,128)}, f32[192,384]{1,0:T(8,128)}) custom-call(bf16[256,3072]{1,0:T(8,128)(2,1)} %tok_hbm.1, bf16[256,3072]{1,0:T(8,128)(2,1)} %cot_hbm.1, bf16[576,384]{1,0:T(8,128)(2,1)} %bitcast.8, bf16[192,384]{1,0:T(8,128)(2,1)} %wo_hbm.1, s32[16]{0:T(128)} %slab.1, ...), custom_call_target="tpu_custom_call" | custom-call | flops 20000000000 | bytes 10000000 | tf_op jit(solution)/shard_map/sublayer/pallas_call | solution.py:794
  136.3 2.6 %deliver.1 = (bf16[256,384]{1,0:T(8,128)(2,1)}, bf16[256,384]{1,0:T(8,128)(2,1)}, f32[576,384]{1,0:T(8,128)}, f32[192,384]{1,0:T(8,128)}) custom-call(bf16[256,384]{1,0:T(8,128)(2,1)} %get-tuple-element.12.refs_0_, bf16[256,384]{1,0:T(8,128)(2,1)} %get-tuple-element.13.refs_1_, f32[576,384]{1,0:T(8,128)} %get-tuple-element.14.refs_2_, ...), custom_call_target="tpu_custom_call" | custom-call | tf_op jit(solution)/shard_map/deliver/pallas_call | solution.py:805

commit v4 on v3

v4 whole, which is shorter than its diff:
```python
import math

import jax
import jax.numpy as jnp
from jax import lax
from jax.experimental import pallas as pl
from jax.experimental.pallas import tpu as pltpu
from jax.sharding import PartitionSpec as P

MESH = pl.DeviceIdType.MESH
HD = 128
NH = 3
ROWS = 256
WID = NH * HD
D = 3072
OWN = 192
EPS = 1e-06
INV_ROOT = 1.0 / math.sqrt(HD)
EXP2_SCALE = INV_ROOT * math.log2(math.e)
BF = jnp.bfloat16
F32 = jnp.float32
GATHER_TWO, GATHER_ONE = range(31), (0, 3, 4, 6, 7, 8, 9, 14, 15, 18, 19, 21, 22, 23, 24, 26, 29)
SUM_TWO, SUM_ONE = range(23), (*range(4, 16), 22)
W_AT, O_AT, KB_AT, KA_AT, DB_AT, GO_AT, DA_AT, OUT_AT, TOK_AT, SEMS = 0, 31, 62, 93, 110, 133, 156, 169, 182, 195
SUM_FIRST = 144
QKV_FIRST, OUT_FIRST, KV_FIRST, DKV_FIRST, KVW_FIRST = 320, 112, 64, 64, 304


def dot(a, b):
    return jnp.dot(a, b, preferred_element_type=F32)


def dot_nt(a, b):
    return lax.dot_general(a, b, (((1,), (1,)), ((), ())), preferred_element_type=F32)


def at_tile(z, x, c):
    return z * 8 + x * 2 + c


class Place:
    def __init__(self):
        t = lax.axis_index("tile")
        self.me = t
        self.z, self.x, self.c = t // 8, (t // 2) % 4, t % 2
        self.xr, self.xl, self.xo = (self.x + 1) % 4, (self.x + 3) % 4, (self.x + 2) % 4
        self.right = at_tile(self.z, self.xr, self.c)
        self.left = at_tile(self.z, self.xl, self.c)
        self.across = at_tile(1 - self.z, self.x, self.c)
        self.sib = at_tile(self.z, self.x, 1 - self.c)


def split_rows(rows, first):
    def halves(start, size, up):
        half = size // 32 * 16 + (16 if up and size % 32 else 0)
        return pl.ds(start, size), (pl.ds(start, half), pl.ds(start + half, size - half))
    a, ah = halves(0, first, True)
    b, bh = halves(first, rows - first, False)
    return a, ah, b, bh


class Sems:
    def __init__(self, send, recv, base, keys):
        self.send, self.recv, self.base, self.keys = send, recv, base, tuple(keys)

    def __call__(self, k):
        i = self.base + self.keys.index(k)
        return dict(send_sem=self.send.at[i], recv_sem=self.recv.at[i])


class Gather:
    def __init__(self, place, buf, first, sems, for_across=None):
        self.p, self.buf, self.sems = place, buf, sems
        self.two, self.for_across = first < buf.shape[1], for_across
        self.a, self.ah, self.b, self.bh = split_rows(buf.shape[1], first)
        self.sent = []

    def copy(self, k, ref, dev):
        return pltpu.make_async_remote_copy(
            src_ref=ref, dst_ref=ref, **self.sems(k), device_id={"tile": dev}, device_id_type=MESH)

    def go(self, k, t, rows, dev):
        c = self.copy(k, self.buf.at[t, rows], dev)
        c.start()
        self.sent.append(c)

    def got(self, k, t, rows):
        self.copy(k, self.buf.at[t, rows], self.p.sib).wait_recv()

    def start(self):
        p = self.p
        if self.two:
            self.go(0, p.me, self.a, p.across)
            self.go(1, p.me, self.b, p.right)
            self.go(2, p.me, self.b, p.left)
        else:
            c = pltpu.make_async_remote_copy(
                src_ref=self.for_across, dst_ref=self.buf.at[p.me], **self.sems(0),
                device_id={"tile": p.across}, device_id_type=MESH)
            c.start()
            self.sent.append(c)
            self.go(3, p.me, self.a, p.right)
            self.go(4, p.me, self.a, p.left)
        c = self.copy(6, self.buf.at[p.me], p.sib)
        c.start()
        self.sent.append(c)

    def start_rest(self, in_turn):
        p = self.p
        if in_turn:
            for c in self.sent[1:3]:
                c.wait_send()
        self.go(3, p.me, self.a, p.right)
        self.go(4, p.me, self.a, p.left)
        if in_turn:
            self.sent[0].wait_send()
            del self.sent[:3]
        self.go(5, p.me, self.b, p.across)

    def step_across(self):
        p = self.p
        self.got(0, p.across, self.a)
        self.go(7, p.across, self.a, p.right)
        self.go(8, p.across, self.a, p.left)
        self.go(9, p.across, self.a, p.sib)

    def step_sides(self):
        p = self.p
        if self.two:
            self.got(1, p.left, self.b)
            self.go(10, p.left, self.bh[0], p.right)
            self.go(11, p.left, self.b, p.across)
            self.got(2, p.right, self.b)
            self.go(12, p.right, self.bh[1], p.left)
            self.go(13, p.right, self.b, p.across)
        self.got(3, p.left, self.a)
        self.go(14, p.left, self.ah[0], p.right)
        self.got(4, p.right, self.a)
        self.go(15, p.right, self.ah[1], p.left)
        if self.two:
            self.go(16, p.left, self.b, p.sib)
            self.go(17, p.right, self.b, p.sib)
        self.go(18, p.left, self.a, p.sib)
        self.go(19, p.right, self.a, p.sib)

    def step_sides_across(self):
        p = self.p
        zl, zr = at_tile(1 - p.z, p.xl, p.c), at_tile(1 - p.z, p.xr, p.c)
        to = at_tile(p.z, p.xo, p.c)
        if self.two:
            self.got(10, to, self.bh[0])
            self.got(12, to, self.bh[1])
            self.go(25, to, self.b, p.across)
        self.got(7, zl, self.a)
        self.go(21, zl, self.ah[0], p.right)
        self.got(8, zr, self.a)
        self.go(22, zr, self.ah[1], p.left)
        self.go(23, zl, self.a, p.sib)
        self.go(24, zr, self.a, p.sib)
        if self.two:
            self.got(5, p.across, self.b)
            self.go(20, p.across, self.b, p.sib)

    def step_opposite(self):
        p = self.p
        zl, zr = at_tile(1 - p.z, p.xl, p.c), at_tile(1 - p.z, p.xr, p.c)
        to = at_tile(p.z, p.xo, p.c)
        self.got(14, to, self.ah[0])
        self.got(15, to, self.ah[1])
        c = self.copy(26, self.buf.at[to], p.sib)
        c.start()
        self.sent.append(c)
        if self.two:
            self.got(11, zl, self.b)
            self.go(27, zl, self.b, p.sib)
            self.got(13, zr, self.b)
            self.go(28, zr, self.b, p.sib)

    def step_last(self):
        p = self.p
        zo = at_tile(1 - p.z, p.xo, p.c)
        self.got(21, zo, self.ah[0])
        self.got(22, zo, self.ah[1])
        self.go(29, zo, self.a, p.sib)
        if self.two:
            self.got(25, zo, self.b)
            self.go(30, zo, self.b, p.sib)

    def sib_own(self):
        self.copy(6, self.buf.at[self.p.sib], self.p.sib).wait_recv()

    def sib_across(self):
        p = self.p
        t = at_tile(1 - p.z, p.x, 1 - p.c)
        self.got(9, t, self.a)
        if self.two:
            self.got(20, t, self.b)

    def sib_sides(self):
        p = self.p
        tl, tr = at_tile(p.z, p.xl, 1 - p.c), at_tile(p.z, p.xr, 1 - p.c)
        if self.two:
            self.got(16, tl, self.b)
            self.got(17, tr, self.b)
        self.got(18, tl, self.a)
        self.got(19, tr, self.a)

    def sib_sides_across(self):
        p = self.p
        zl, zr = at_tile(1 - p.z, p.xl, 1 - p.c), at_tile(1 - p.z, p.xr, 1 - p.c)
        self.got(23, zl, self.a)
        self.got(24, zr, self.a)
        if self.two:
            self.got(27, zl, self.b)
            self.got(28, zr, self.b)

    def sib_opposite(self):
        p = self.p
        self.copy(26, self.buf.at[at_tile(p.z, p.xo, 1 - p.c)], p.sib).wait_recv()

    def sib_last(self):
        p = self.p
        zo = at_tile(1 - p.z, p.xo, 1 - p.c)
        self.got(29, zo, self.a)
        if self.two:
            self.got(30, zo, self.b)

    def finish(self):
        for c in self.sent:
            c.wait_send()


class Scatter:
    def __init__(self, axis, ring, pair, devices, parts, first, bufs, sems):
        self.axis, self.ring, self.pair = axis, ring, pair
        self.right, self.left, self.across = devices
        self.parts = parts
        self.far, self.near, self.last = bufs[:3]
        self.zed, self.far_b, self.near_b = bufs[3:] if len(bufs) > 3 else (None, None, None)
        self.sems = sems
        self.rr, self.rl, self.ro = (ring + 1) % 4, (ring + 3) % 4, (ring + 2) % 4
        self.a, self.ah, self.b, self.bh = split_rows(parts.shape[2], first)
        self.first = first
        self.bl = [pl.ds(h.start - first, h.size) for h in self.bh]
        self.sent = []

    def copy(self, k, src, dst, dev):
        return pltpu.make_async_remote_copy(
            src_ref=src, dst_ref=dst, **self.sems(k), device_id={self.axis: dev}, device_id_type=MESH)

    def go(self, k, src, dst, dev):
        c = self.copy(k, src, dst, dev)
        c.start()
        self.sent.append(c)

    def got(self, k, dst):
        self.copy(k, dst, dst, self.right).wait_recv()

    def add(self, ring, pair, rows, got):
        self.parts[ring, pair, rows] = (
            self.parts[ring, pair, rows].astype(F32) + got.astype(F32)).astype(BF)


    def pairs(self):
        return (0, 1 - self.pair), (1, self.pair)

    def start_z(self, k, ring):
        if self.zed is not None:
            self.go(k, self.parts.at[ring, 1 - self.pair, self.b], self.zed.at[ring], self.across)

    def got_z(self, k, ring):
        self.got(k, self.zed.at[ring])

    def far_at(self, i, n):
        return self.far.at[i, n, pl.ds(0, self.ah[i].size)]

    def start_far(self, n, over=True):
        z = self.pairs()[n][1]
        for i, dev in enumerate((self.right, self.left)):
            self.go(4 + 2 * n + i, self.parts.at[self.ro, z, self.ah[i]], self.far_at(i, n), dev)
        if n == 0 and over:
            self.start_z(0, self.ro)

    def start_near(self, n, over=True):
        z = self.pairs()[n][1]
        for i, (ring, dev) in enumerate(((self.rr, self.right), (self.rl, self.left))):
            rows = self.ah[1 - i]
            self.go(8 + 2 * n + i, self.parts.at[ring, z, rows], self.near.at[i, n, rows], dev)
            if n == 0 and over:
                self.start_z(1 + i, ring)

    def start_own(self):
        self.start_z(3, self.ring)

    def start_over(self):
        for k, ring in enumerate((self.ro, self.rr, self.rl, self.ring)):
            self.start_z(k, ring)

    def step_far_b(self):
        self.got_z(0, self.ro)
        self.add(self.ro, self.pair, self.b, self.zed[self.ro])
        for i, dev in enumerate((self.right, self.left)):
            self.go(16 + i, self.parts.at[self.ro, self.pair, self.bh[i]], self.far_b.at[i, pl.ds(0, self.bh[i].size)], dev)

    def step_near(self, n):
        z = self.pairs()[n][1]
        for i, (ring, dev) in enumerate(((self.rr, self.right), (self.rl, self.left))):
            rows, got = self.ah[i], self.far_at(i, n)
            self.got(4 + 2 * n + i, got)
            self.add(ring, z, rows, got[...])
            self.go(12 + 2 * n + i, self.parts.at[ring, z, rows], self.near.at[i, n, rows], dev)

    def step_near_b(self):
        for i, (ring, dev) in enumerate(((self.rr, self.right), (self.rl, self.left))):
            self.got_z(1 + i, ring)
            self.add(ring, self.pair, self.b, self.zed[ring])
            j = 1 - i
            self.go(18 + i, self.parts.at[ring, self.pair, self.bh[j]], self.near_b.at[i, self.bl[j]], dev)
        for i, (ring, dev) in enumerate(((self.rr, self.right), (self.rl, self.left))):
            got = self.far_b.at[i, pl.ds(0, self.bh[i].size)]
            self.got(16 + i, got)
            self.add(ring, self.pair, self.bh[i], got[...])
            self.go(20 + i, self.parts.at[ring, self.pair, self.bh[i]], self.near_b.at[i, self.bl[i]], dev)

    def total(self, n):
        for i in range(2):
            self.got(8 + 2 * n + i, self.near.at[i, n, self.ah[1 - i]])
            self.got(12 + 2 * n + i, self.near.at[i, n, self.ah[i]])
        z = self.pairs()[n][1]
        return (self.parts[self.ring, z, self.a].astype(F32) + self.near[0, n].astype(F32)
                + self.near[1, n].astype(F32))

    def step_pair(self):
        other = 1 - self.pair
        self.parts[self.ring, other, self.a] = self.total(0).astype(BF)
        self.go(22, self.parts.at[self.ring, other, self.a], self.last, self.across)

    def result_b(self, out):
        self.got_z(3, self.ring)
        for i in range(2):
            self.got(18 + i, self.near_b.at[i, self.bl[1 - i]])
            self.got(20 + i, self.near_b.at[i, self.bl[i]])
        out[self.b] = (
            (self.parts[self.ring, self.pair, self.b].astype(F32) + self.zed[self.ring].astype(F32))
            + (self.near_b[0].astype(F32) + self.near_b[1].astype(F32))).astype(out.dtype)

    def result_own(self, out):
        out[...] = self.total(1)

    def result_last(self, out):
        self.got(22, self.last)
        out[...] = self.last[...].astype(F32)

    def result_a(self, out):
        own = self.total(1)
        self.got(22, self.last)
        out[self.a] = (own + self.last[...].astype(F32)).astype(out.dtype)

    def finish(self):
        for c in self.sent:
            c.wait_send()


def kernel(tok_hbm, cot_hbm, w_hbm, wo_hbm, slab, ext,
           out_ref, gtok_ref, gqkv_ref, gout_ref,
           w, wo, kva, kvb, kv_out, tok, cot, tok_t, tok_sib, cot_t, cot_sib, wexp, mask,
           proj, q, qt, g_all, g, gt, num, den, delta, dq, att, gp, dkv_sum, pair_out, pair_in,
           d_out, d_parts, da_far, da_near, da_last, db_far, db_near, db_last, db_zed, db_far_b, db_near_b,
           gq_parts, gq_far, gq_near, gq_last, gq_zed, gq_far_b, gq_near_b,
           gk_parts, gk_far, gk_near, gk_last, gk_zed, gk_far_b, gk_near_b,
           go_parts, go_far, go_near, go_last, go_zed, go_far_b, go_near_b,
           ho_parts, ho_far, ho_near, ho_last, ht_parts, ht_far, ht_near, ht_last,
           load_sem, lane_send, lane_recv, sib_send, sib_recv, dkv_send, dkv_recv, pair_send, pair_recv):
    p = Place()
    hd = lax.axis_index("head")
    hy, hz = hd // 2, hd % 2
    head_devices = (((hy + 1) % 4) * 2 + hz, ((hy + 3) % 4) * 2 + hz, hy * 2 + 1 - hz)
    lane_devices = (p.right, p.left, p.across)

    loads = [pltpu.make_async_copy(a, b, load_sem.at[i]) for i, (a, b) in enumerate((
        (w_hbm, w.at[p.me]), (wo_hbm, wo.at[p.me]), (tok_hbm, tok), (cot_hbm, cot)))]
    for c in loads:
        c.start()

    barrier = pltpu.get_barrier_semaphore()
    for dev in (p.right, p.left, p.across, p.sib):
        pl.semaphore_signal(barrier, inc=1, device_id={"tile": dev}, device_id_type=MESH)
    for dev in head_devices:
        pl.semaphore_signal(barrier, inc=1, device_id={"head": dev}, device_id_type=MESH)
    pl.semaphore_wait(barrier, 7)

    sent = []

    def to_sibling(k, src, dst):
        c = pltpu.make_async_remote_copy(
            src_ref=src, dst_ref=dst, send_sem=sib_send.at[k], recv_sem=sib_recv.at[k],
            device_id={"tile": p.sib}, device_id_type=MESH)
        c.start()
        sent.append(c)
        return c

    def sems(base, keys):
        return Sems(lane_send, lane_recv, base, keys)

    gather_w = Gather(p, w, QKV_FIRST, sems(W_AT, GATHER_TWO))
    gather_o = Gather(p, wo, OUT_FIRST, sems(O_AT, GATHER_TWO))
    head_a, head_x = 2 * p.z, 2 * (1 - p.z)
    row_0 = p.z == 0

    def of_a(get):
        return jnp.where(row_0, get(slice(0, HD)), get(slice(2 * HD, 3 * HD)))

    def of_x(get):
        return jnp.where(row_0, get(slice(2 * HD, 3 * HD)), get(slice(0, HD)))

    def of_b(get):
        return get(slice(HD, 2 * HD))

    def wide(ref, *index):
        return jnp.concatenate([ref[(*index, h)] for h in range(NH)], axis=1)

    def to_across(k, dst):
        c = pltpu.make_async_remote_copy(
            src_ref=pair_out.at[k], dst_ref=dst, send_sem=pair_send.at[k], recv_sem=pair_recv.at[k],
            device_id={"tile": p.across}, device_id_type=MESH)
        c.start()
        sent.append(c)
        return c

    gather_ka = Gather(p, kva, ROWS, sems(KA_AT, GATHER_ONE), kv_out)
    gather_kb = Gather(p, kvb, KV_FIRST, sems(KB_AT, GATHER_TWO))
    scatter = lambda base, parts, first, *bufs: Scatter(
        "tile", p.x, p.z, lane_devices, parts, first, bufs, sems(base, SUM_TWO if len(bufs) > 3 else SUM_ONE))
    head_scatter = lambda base, parts, *bufs: Scatter(
        "head", hy, hz, head_devices, parts, ROWS, bufs, sems(base, SUM_ONE))
    sum_da = Scatter("tile", 0, 0, lane_devices, d_parts.at[0], ROWS, (da_far, da_near, da_last), sems(DA_AT, SUM_ONE))
    sum_db = Scatter("tile", 0, 0, lane_devices, d_parts.at[1], DKV_FIRST,
                     (db_far, db_near, db_last, db_zed, db_far_b, db_near_b), sems(DB_AT, SUM_TWO))
    sum_gk = scatter(W_AT, gk_parts, KVW_FIRST, gk_far, gk_near, gk_last, gk_zed, gk_far_b, gk_near_b)
    sum_gq = scatter(O_AT, gq_parts, SUM_FIRST, gq_far, gq_near, gq_last, gq_zed, gq_far_b, gq_near_b)
    sum_go = scatter(GO_AT, go_parts, SUM_FIRST, go_far, go_near, go_last, go_zed, go_far_b, go_near_b)
    sum_out = head_scatter(OUT_AT, ho_parts, ho_far, ho_near, ho_last)
    sum_tok = head_scatter(TOK_AT, ht_parts, ht_far, ht_near, ht_last)

    loads[0].wait()
    gather_w.start()

    height = lax.rem(slab[p.me], 4)
    near_height = lax.rem(slab[p.sib], 4)
    far_height = lax.rem(slab[at_tile(p.z, p.xr, 1 - p.c)], 4)
    key_width = lax.broadcasted_iota(jnp.int32, (64, ROWS), 1) // 64
    for qw in range(4):
        reach_h = ext[0, height * 4 + qw]
        reach_w = ext[1, height * 4 + qw]
        near_w = jnp.where(jnp.abs(key_width - qw) <= reach_w, 1.0, 0.0)
        for m, other in enumerate((height, near_height, far_height)):
            gap = jnp.full((64, ROWS), jnp.abs(height - other), jnp.int32)
            mask[m, qw * 64:(qw + 1) * 64] = jnp.where(gap <= reach_h, near_w, 0.0)

    loads[2].wait()
    loads[3].wait()

    def turn(src, dst):
        def body(j, carry):
            cols = pl.ds(pl.multiple_of(j * 384, 384), 384)
            dst[j] = src[:, cols].T.reshape(2, OWN, ROWS)
            return carry
        lax.fori_loop(0, 8, body, 0)

    turn(tok, tok_t)
    tok_swap = to_sibling(0, tok_t.at[:, 1 - p.c], tok_sib)
    turn(cot, cot_t)
    cot_swap = to_sibling(1, cot_t.at[:, 1 - p.c], cot_sib)

    def project(z, x):
        j = z * 4 + x
        t = tok[:, pl.ds(pl.multiple_of(j * 384, 384), 384)]

        def one(i, carry):
            rows = pl.ds(pl.multiple_of(i * OWN, OWN), OWN)
            proj[i] += dot(t, w[pl.ds(2 * j, 2), rows, :].reshape(2 * OWN, WID))
            return carry
        lax.fori_loop(0, 3, one, 0)

    proj[...] = jnp.zeros_like(proj)
    gather_w.start_rest(True)
    gather_w.step_across()
    gather_w.sib_own()
    project(p.z, p.x)
    gather_w.step_sides()
    loads[1].wait()
    gather_o.start()
    gather_o.start_rest(False)
    gather_w.sib_sides()
    project(p.z, p.xl)
    project(p.z, p.xr)
    gather_w.step_sides_across()
    gather_o.step_across()
    gather_w.sib_across()
    project(1 - p.z, p.x)
    gather_w.step_opposite()
    gather_w.sib_sides_across()
    project(1 - p.z, p.xl)
    project(1 - p.z, p.xr)
    gather_w.step_last()
    gather_o.step_sides()
    gather_w.sib_opposite()
    project(p.z, p.xo)
    gather_w.sib_last()
    project(1 - p.z, p.xo)

    def scale_of(raw):
        return lax.rsqrt(jnp.mean(raw * raw, axis=-1, keepdims=True) + EPS)

    def head_of(of, i):
        return of(lambda cols: proj[i, :, cols])

    def unit_rows(of, i):
        raw = head_of(of, i)
        return (raw * scale_of(raw)).astype(BF)

    kv_out[:, :HD] = unit_rows(of_x, 1)
    kv_out[:, HD:] = head_of(of_x, 2).astype(BF)
    kva[p.me, :, :HD] = unit_rows(of_a, 1)
    kva[p.me, :, HD:] = head_of(of_a, 2).astype(BF)
    gather_ka.start()
    kvb[p.me, :, :HD] = unit_rows(of_b, 1)
    kvb[p.me, :, HD:] = head_of(of_b, 2).astype(BF)
    gather_kb.start()
    pair_out[0] = unit_rows(of_x, 0)
    q_pair = to_across(0, q.at[1])
    gather_kb.start_rest(False)
    q[0] = unit_rows(of_a, 0)
    q[2] = unit_rows(of_b, 0)
    for u in (0, 2):
        qt[u] = q[u].T

    def block(fn, *args):
        pl.when(p.me >= 0)(lambda: fn(*args))

    def forward(t, m, i, units=(0, 1, 2), first=False):
        block(forward_block, t, m, i, units, first)

    def forward_block(t, m, i, units, first):
        for u in units:
            kv = kva if u < 2 else kvb
            scores = dot_nt(q[u], kv[t, :, :HD])
            we = jnp.exp2(scores * EXP2_SCALE) * mask[m]
            wexp[i, u] = we
            part = we[:, :HD] + we[:, HD:]
            val = dot(we.astype(BF), kv[t, :, HD:])
            if first:
                den[u] = part
                num[u] = val
            else:
                den[u] += part
                num[u] += val

    def loop2(fn):
        lax.fori_loop(0, 2, lambda i, carry: (fn(i), carry)[1], 0)

    def grad_att(j, acc):
        cols = pl.ds(pl.multiple_of(j * 384, 384), 384)
        return acc + dot(cot[:, cols], wo[pl.ds(2 * j, 2)].reshape(2 * OWN, WID))

    def two(first, second):
        forward(*first)
        forward(*second)

    def side(zz, i):
        two((at_tile(zz, p.xl, 1 - p.c), 2, 4 + 2 * i), (at_tile(zz, p.xr, 1 - p.c), 2, 5 + 2 * i))

    forward(p.me, 0, 0, (0, 2), True)
    gather_o.step_sides_across()
    gather_ka.step_across()
    gather_kb.step_across()
    gather_o.step_opposite()
    gather_ka.sib_own()
    gather_kb.sib_own()
    q_pair.wait_recv()
    qt[1] = q[1].T
    forward(p.me, 0, 0, (1,), True)
    forward(p.sib, 1, 2)
    gather_kb.step_sides()
    gather_ka.step_sides()
    gather_ka.step_sides_across()
    gather_kb.step_sides_across()
    forward(p.across, 0, 1)
    gather_o.step_last()
    gather_ka.sib_sides()
    gather_kb.sib_sides()
    side(p.z, 0)
    gather_ka.step_opposite()
    gather_kb.step_opposite()
    gather_ka.sib_across()
    gather_kb.sib_across()
    two((at_tile(1 - p.z, p.x, 1 - p.c), 1, 3), (at_tile(p.z, p.xo, p.c), 0, 8))
    gather_o.sib_own()
    gather_o.sib_across()
    gather_o.sib_sides()
    gather_o.sib_sides_across()
    gather_o.sib_opposite()
    gather_o.sib_last()
    g_all[...] = lax.fori_loop(0, 8, grad_att, jnp.zeros((ROWS, WID), F32)).astype(BF)
    pair_out[1] = of_x(lambda cols: g_all[:, cols])
    g_pair = to_across(1, g.at[1])
    gather_ka.step_last()
    gather_kb.step_last()
    gather_ka.sib_sides_across()
    gather_kb.sib_sides_across()
    side(1 - p.z, 1)
    g[0] = of_a(lambda cols: g_all[:, cols])
    g[2] = of_b(lambda cols: g_all[:, cols])
    for u in (0, 2):
        gt[u] = g[u].T
    gather_ka.sib_opposite()
    gather_kb.sib_opposite()
    two((at_tile(p.z, p.xo, 1 - p.c), 1, 10), (at_tile(1 - p.z, p.xo, p.c), 0, 9))
    gather_ka.sib_last()
    gather_kb.sib_last()
    forward(at_tile(1 - p.z, p.xo, 1 - p.c), 1, 11)
    g_pair.wait_recv()
    gt[1] = g[1].T

    for u in (1, 0, 2):
        inverse = 1.0 / jnp.sum(den[u], axis=-1, keepdims=True)
        context = num[u] * inverse
        if u == 1:
            pair_out[2] = context.astype(BF)
            att_pair = to_across(2, pair_in.at[0])
        else:
            att[0, head_a if u == 0 else 1] = context.astype(BF)
        row = jnp.sum(g[u].astype(F32) * context, axis=-1, keepdims=True)
        delta[u] = jnp.broadcast_to(row, (ROWS, HD))
        den[u] = jnp.broadcast_to(inverse, (ROWS, HD))

    def backward(t, i, x, z, own):
        block(backward_block, t, i, x, z, own)

    def backward_block(t, i, x, z, own):
        dk, dv = [], []
        for u in range(NH):
            kv = kva if u < 2 else kvb
            grad = dot_nt(g[u], kv[t, :, HD:])
            inverse, row = den[u], delta[u]
            probs, ds = [], []
            for part in range(2):
                cs = slice(part * HD, (part + 1) * HD)
                pr = wexp[i, u, :, cs] * inverse
                ds.append((pr * (grad[:, cs] - row)).astype(BF))
                probs.append(pr.astype(BF))
            probs = jnp.concatenate(probs, axis=1)
            ds = jnp.concatenate(ds, axis=1)
            dq[u] += dot(ds, kv[t, :, :HD])
            dk.append(dot(qt[u], ds))
            dv.append(dot(gt[u], probs))
        for n, ks, vs in ((0, dk[0] + dk[1], dv[0] + dv[1]), (1, dk[2], dv[2])):
            ks = ks * INV_ROOT
            if own:
                ks = ks + d_parts[n, x, z, :HD].astype(F32)
                vs = vs + d_parts[n, x, z, HD:].astype(F32)
            out = d_parts if own else d_out
            out[n, x, z, :HD] = ks.astype(BF)
            out[n, x, z, HD:] = vs.astype(BF)

    def swap_copy(x, z, k):
        return pltpu.make_async_remote_copy(
            src_ref=d_out.at[:, x, z], dst_ref=d_parts.at[:, x, z], send_sem=dkv_send.at[k], recv_sem=dkv_recv.at[k],
            device_id={"tile": p.sib}, device_id_type=MESH)

    def swap(x, z, k):
        c = swap_copy(x, z, k)
        c.start()
        sent.append(c)

    def swapped(x, z, k):
        swap_copy(x, z, k).wait_recv()

    def out_part(ring):
        def one(i):
            o = wo[pl.ds(4 * ring + 2 * i, 2)].reshape(2 * OWN, WID)
            ho_parts[ring, i] = dot_nt(wide(att, 0), o).astype(BF)
        loop2(one)

    def tok_part(ring):
        def one(i):
            j = 2 * ring + i
            acc = dot_nt(wide(gp, 0, 0), w[pl.ds(2 * j, 2), 0:OWN, :].reshape(2 * OWN, WID))
            for n in range(1, 3):
                acc += dot_nt(wide(gp, 0, n), w[pl.ds(2 * j, 2), n * OWN:(n + 1) * OWN, :].reshape(2 * OWN, WID))
            ht_parts[ring, i] = acc.astype(BF)
        loop2(one)

    def out_grad(ring):
        def one(i):
            j = 4 * i + ring
            go_parts[ring, i] = (dot(cot_t[j, p.c], wide(att, 0)) + dot(cot_sib[j], wide(att, 1))).astype(BF)
        loop2(one)

    def qkv_grad(parts, j, which):
        for n, i in enumerate(which):
            parts[j % 4, j // 4, n * OWN:(n + 1) * OWN] = (
                dot(tok_t[j, p.c], wide(gp, 0, i)) + dot(tok_sib[j], wide(gp, 1, i))).astype(BF)

    def kv_grad(ring):
        loop2(lambda i: qkv_grad(gk_parts, i * 4 + ring, (1, 2)))

    def opposite_sib(i):
        zz = (p.z + i) % 2
        backward(at_tile(zz, p.xo, 1 - p.c), 10 + i, 2, i, False)

    def opposite_own(i):
        zz = (p.z + i) % 2
        backward(at_tile(zz, p.xo, p.c), 8 + i, 2, i, True)

    def sides_sib(i):
        zz = (p.z + 1 + i) % 2
        backward(at_tile(zz, p.xl, 1 - p.c), 6 - 2 * i, 3, 1 - i, False)
        backward(at_tile(zz, p.xr, 1 - p.c), 7 - 2 * i, 1, 1 - i, False)

    def own_sib(i):
        zz = (p.z + i) % 2
        backward(at_tile(zz, p.x, 1 - p.c), 2 + i, 0, i, False)

    def own_own(i):
        zz = (p.z + i) % 2
        backward(at_tile(zz, p.x, p.c), i, 0, i, True)

    def unit_back(grad, raw):
        scale = scale_of(raw)
        unit = raw * scale
        return scale * (grad - unit * jnp.mean(grad * unit, axis=-1, keepdims=True))

    dq[...] = jnp.zeros_like(dq)
    opposite_sib(1)
    swap(2, 1, 0)
    opposite_sib(0)
    swap(2, 0, 1)
    swapped(2, 1, 0)
    opposite_own(1)
    sum_da.start_far(0)
    sum_db.start_far(0)
    swapped(2, 0, 1)
    opposite_own(0)
    sum_da.start_far(1)
    sum_db.start_far(1)
    att_pair.wait_recv()
    att[0, head_x] = pair_in[0]
    att_swap = to_sibling(2, att.at[0], att.at[1])
    sides_sib(0)
    swap(3, 1, 2)
    swap(1, 1, 3)
    cot_swap.wait_recv()
    att_swap.wait_recv()
    out_grad(p.xo)
    sum_go.start_far(0, False)
    sum_go.start_far(1, False)
    sides_sib(1)
    swap(3, 0, 4)
    swap(1, 0, 5)
    out_part(sum_out.ro)
    sum_out.start_far(0)
    sum_out.start_far(1)
    swapped(3, 1, 2)
    swapped(1, 1, 3)
    sum_da.start_near(0)
    sum_db.start_near(0)
    out_part(sum_out.rr)
    out_part(sum_out.rl)
    sum_out.start_near(0)
    sum_out.start_near(1)
    swapped(3, 0, 4)
    swapped(1, 0, 5)
    sum_da.start_near(1)
    sum_db.start_near(1)
    sum_da.step_near(0)
    sum_db.step_far_b()
    out_grad(p.xr)
    out_grad(p.xl)
    sum_go.start_z(0, p.xo)
    sum_go.start_z(1, p.xr)
    sum_go.start_z(2, p.xl)
    loop2(own_sib)
    swap(0, 0, 6)
    swap(0, 1, 7)
    sum_db.step_near(0)
    sum_da.step_near(1)
    sum_db.step_near(1)
    swapped(0, 0, 6)
    swapped(0, 1, 7)
    loop2(own_own)
    sum_db.start_own()
    pair_out[3] = dq[1].astype(BF)
    dq_pair = to_across(3, pair_in.at[1])
    out_grad(p.x)
    sum_db.step_near_b()
    sum_go.start_near(0, False)
    sum_go.start_near(1, False)
    sum_go.step_near(0)
    sum_go.step_near(1)
    sum_go.start_own()
    out_part(sum_out.ring)
    sum_da.step_pair()
    sum_db.step_pair()

    def head_grad(i, of, head, grad):
        gp[0, i, head] = unit_back(grad, head_of(of, i)).astype(BF)

    head_grad(0, of_a, head_a, dq[0] * INV_ROOT)
    head_grad(0, of_b, 1, dq[2] * INV_ROOT)
    dq_pair.wait_recv()
    head_grad(0, of_x, head_x, pair_in[1].astype(F32) * INV_ROOT)
    gq_swap = to_sibling(3, gp.at[0, 0], gp.at[1, 0])
    sum_out.step_near(0)
    sum_out.step_near(1)

    tok_swap.wait_recv()
    gq_swap.wait_recv()
    lax.fori_loop(0, 8, lambda j, carry: (qkv_grad(gq_parts, j, (0,)), carry)[1], 0)
    gather_w.finish()
    gather_o.finish()
    sum_gq.start_far(0, False)
    sum_gq.start_far(1, False)
    sum_gq.start_near(0, False)
    sum_gq.start_near(1, False)
    sum_gq.start_over()

    def kv_head(n, of, head):
        head_grad(1, of, head, dkv_sum[n, :HD].T)
        gp[0, 2, head] = dkv_sum[n, HD:].T.astype(BF)

    sum_da.result_own(dkv_sum.at[0])
    kv_head(0, of_a, head_a)
    sum_db.result_b(dkv_sum.at[1])
    sum_db.result_a(dkv_sum.at[1])
    kv_head(1, of_b, 1)
    sum_da.result_last(dkv_sum.at[2])
    kv_head(2, of_x, head_x)
    gk_swap = to_sibling(4, gp.at[0, pl.ds(1, 2)], gp.at[1, pl.ds(1, 2)])

    sum_out.step_pair()
    sum_go.step_far_b()
    tok_part(sum_tok.ro)
    sum_tok.start_far(0)
    sum_tok.start_far(1)
    gk_swap.wait_recv()
    kv_grad(p.xo)
    sum_gk.start_far(0)
    sum_gk.start_far(1)
    sum_go.step_pair()
    sum_gq.step_near(0)
    sum_gq.step_near(1)
    sum_go.step_near_b()
    tok_part(sum_tok.rr)
    tok_part(sum_tok.rl)
    sum_tok.start_near(0)
    sum_tok.start_near(1)
    kv_grad(p.xr)
    kv_grad(p.xl)
    sum_gk.start_near(0)
    sum_gk.start_near(1)
    sum_gq.step_far_b()
    tok_part(sum_tok.ring)
    sum_tok.step_near(0)
    sum_tok.step_near(1)
    kv_grad(p.x)
    sum_gk.start_own()
    sum_gk.step_near(0)
    sum_gk.step_near(1)
    sum_gk.step_far_b()
    sum_gq.step_near_b()
    sum_out.result_a(out_ref)
    sum_go.result_b(gout_ref)
    sum_go.result_a(gout_ref)
    sum_tok.step_pair()
    sum_gq.step_pair()
    sum_gk.step_near_b()
    sum_gk.step_pair()
    sum_gq.result_b(gqkv_ref.at[pl.ds(0, OWN)])
    sum_gq.result_a(gqkv_ref.at[pl.ds(0, OWN)])
    sum_tok.result_a(gtok_ref)
    sum_gk.result_b(gqkv_ref.at[pl.ds(OWN, 2 * OWN)])
    sum_gk.result_a(gqkv_ref.at[pl.ds(OWN, 2 * OWN)])

    for s in (gather_ka, gather_kb, sum_da, sum_db, sum_gq, sum_gk, sum_go, sum_out, sum_tok):
        s.finish()
    for c in sent:
        c.wait_send()


def lane_bufs(rows, first, cols):
    _, ah, _, bh = split_rows(rows, first)
    second = rows - first
    bufs = [(2, 2, ah[0].size, cols), (2, 2, first, cols), (first, cols)]
    if second:
        bufs += [(4, second, cols), (2, bh[1].size, cols), (2, second, cols)]
    return [pltpu.VMEM(b, BF) for b in bufs]


def deliver(*refs):
    for i in range(4):
        refs[4 + i][...] = refs[i][...]


def local(tokens, cotangent, qkv_weight, out_weight, slab_of_device, extents):
    w = jnp.transpose(qkv_weight, (1, 0, 2)).reshape(3 * OWN, WID)
    vm = lambda *shape, dtype=BF: pltpu.VMEM(shape, dtype)
    dma = lambda *shape: pltpu.SemaphoreType.DMA(shape)
    scratch = [
        vm(16, 3 * OWN, WID), vm(16, OWN, WID), vm(16, ROWS, ROWS), vm(16, ROWS, ROWS), vm(ROWS, ROWS), vm(ROWS, D), vm(ROWS, D),
        vm(8, 2, OWN, ROWS), vm(8, OWN, ROWS), vm(8, 2, OWN, ROWS), vm(8, OWN, ROWS),
        vm(12, NH, ROWS, ROWS, dtype=F32), vm(3, ROWS, ROWS, dtype=F32),
        vm(3, ROWS, WID, dtype=F32), vm(NH, ROWS, HD), vm(NH, HD, ROWS),
        vm(ROWS, WID), vm(NH, ROWS, HD), vm(NH, HD, ROWS),
        vm(NH, ROWS, HD, dtype=F32), vm(NH, ROWS, HD, dtype=F32), vm(NH, ROWS, HD, dtype=F32),
        vm(NH, ROWS, HD, dtype=F32), vm(2, NH, ROWS, HD), vm(2, 3, NH, ROWS, HD), vm(NH, ROWS, ROWS, dtype=F32),
        vm(4, ROWS, HD), vm(2, ROWS, HD),
        vm(2, 4, 2, ROWS, ROWS), vm(2, 4, 2, ROWS, ROWS),
        *lane_bufs(ROWS, ROWS, ROWS), *lane_bufs(ROWS, DKV_FIRST, ROWS),
        vm(4, 2, OWN, WID), *lane_bufs(OWN, SUM_FIRST, WID),
        vm(4, 2, 2 * OWN, WID), *lane_bufs(2 * OWN, KVW_FIRST, WID),
        vm(4, 2, OWN, WID), *lane_bufs(OWN, SUM_FIRST, WID),
        vm(4, 2, ROWS, WID), *lane_bufs(ROWS, ROWS, WID), vm(4, 2, ROWS, WID), *lane_bufs(ROWS, ROWS, WID),
        dma(4), dma(SEMS), dma(SEMS), dma(5), dma(5), dma(8), dma(8), dma(4), dma(4),
    ]
    any_spec = pl.BlockSpec(memory_space=pl.ANY)
    smem = pl.BlockSpec(memory_space=pltpu.SMEM)
    vmem = pl.BlockSpec(memory_space=pltpu.VMEM)
    shapes = (
        jax.ShapeDtypeStruct((ROWS, WID), BF), jax.ShapeDtypeStruct((ROWS, WID), BF),
        jax.ShapeDtypeStruct((3 * OWN, WID), F32), jax.ShapeDtypeStruct((OWN, WID), F32))
    results = pl.pallas_call(
        kernel,
        out_shape=shapes,
        in_specs=[any_spec] * 4 + [smem] * 2,
        out_specs=(vmem,) * 4,
        scratch_shapes=scratch,
        compiler_params=pltpu.CompilerParams(
            collective_id=0, has_side_effects=True, vmem_limit_bytes=64 * 1024 * 1024),
        cost_estimate=pl.CostEstimate(flops=20_000_000_000, bytes_accessed=10_000_000, transcendentals=2_400_000),
        name="sublayer",
    )(tokens, cotangent, w, out_weight, slab_of_device, extents.T)
    output, grad_tokens, grad_qkv, grad_out = pl.pallas_call(
        deliver, out_shape=shapes, in_specs=[vmem] * 4, out_specs=(vmem,) * 4, name="deliver")(*results)
    grad_qkv = jnp.transpose(grad_qkv.reshape(3, OWN, WID), (1, 0, 2))
    return output, grad_tokens, grad_qkv, grad_out


def solution(mesh):
    return jax.shard_map(
        local, mesh=mesh,
        in_specs=(P("tile", None), P("tile", None), P("tile", None, "head"), P("tile", "head"), P(None), P(None, None)),
        out_specs=(P("tile", "head"), P("tile", "head"), P("tile", None, "head"), P("tile", "head")),
        check_vma=False)
```

time: 139 us -> 128 us (0.921)
  Pallas kernels: 138 us -> 127 us
    pallas_call x1, Pallas kernels: 136 us -> 124 us  [local(): pl.pallas_call(kernel, out_shape=shapes, in_specs=[any_spec] * 4 + [smem]...]
where the time goes in v4:
time: 128 us
  Pallas kernels  127 us (99%)
    pallas_call x1, Pallas kernels, local(): pl.pallas_call(kernel, out_shape=shapes, in_specs=[any_spec] * 4 + [smem]...  124 us
    pallas_call x1, Pallas kernels, local(): pl.pallas_call(deliver, out_shape=shapes, in_specs=[vmem] * 4, out_specs=...  2.58 us

profile of v4, /device:TPU:1, one launch (start us, length us, event | category | flops | bytes accessed | tf_op | source)
XLA Modules:
  0.0 127.5 jit_solution(15800460246479838161)
XLA Ops:
  0.6 124.3 %sublayer.1 = (bf16[256,384]{1,0:T(8,128)(2,1)}, bf16[256,384]{1,0:T(8,128)(2,1)}, f32[576,384]{1,0:T(8,128)}, f32[192,384]{1,0:T(8,128)}) custom-call(bf16[256,3072]{1,0:T(8,128)(2,1)} %tok_hbm.1, bf16[256,3072]{1,0:T(8,128)(2,1)} %cot_hbm.1, bf16[576,384]{1,0:T(8,128)(2,1)} %bitcast.8, bf16[192,384]{1,0:T(8,128)(2,1)} %wo_hbm.1, s32[16]{0:T(128)} %slab.1, ...), custom_call_target="tpu_custom_call" | custom-call | flops 20000000000 | bytes 10000000 | tf_op jit(solution)/shard_map/sublayer/pallas_call | solution.py:932
  124.9 2.6 %deliver.1 = (bf16[256,384]{1,0:T(8,128)(2,1)}, bf16[256,384]{1,0:T(8,128)(2,1)}, f32[576,384]{1,0:T(8,128)}, f32[192,384]{1,0:T(8,128)}) custom-call(bf16[256,384]{1,0:T(8,128)(2,1)} %get-tuple-element.12.refs_0_, bf16[256,384]{1,0:T(8,128)(2,1)} %get-tuple-element.13.refs_1_, f32[576,384]{1,0:T(8,128)} %get-tuple-element.14.refs_2_, ...), custom_call_target="tpu_custom_call" | custom-call | tf_op jit(solution)/shard_map/deliver/pallas_call | solution.py:943

commit v5 on v4

--- a/solution.py
+++ b/solution.py
@@ -476,11 +476,8 @@
         j = z * 4 + x
         t = tok[:, pl.ds(pl.multiple_of(j * 384, 384), 384)]
 
-        def one(i, carry):
-            rows = pl.ds(pl.multiple_of(i * OWN, OWN), OWN)
-            proj[i] += dot(t, w[pl.ds(2 * j, 2), rows, :].reshape(2 * OWN, WID))
-            return carry
-        lax.fori_loop(0, 3, one, 0)
+        for i in range(3):
+            proj[i] += dot(t, w[pl.ds(2 * j, 2), i * OWN:(i + 1) * OWN, :].reshape(2 * OWN, WID))
 
     proj[...] = jnp.zeros_like(proj)
     gather_w.start_rest(True)

time: 128 us -> 127 us (level)
  no operation moved by 1% of the time
where the time goes in v5:
time: 127 us; the launch traced here: 126 us
  Pallas kernels  126 us (99%)
    pallas_call x1, Pallas kernels, local(): pl.pallas_call(kernel, out_shape=shapes, in_specs=[any_spec] * 4 + [smem]...  123 us
    pallas_call x1, Pallas kernels, local(): pl.pallas_call(deliver, out_shape=shapes, in_specs=[vmem] * 4, out_specs=...  2.58 us

profile of v5, /device:TPU:1, one launch (start us, length us, event | category | flops | bytes accessed | tf_op | source)
XLA Modules:
  0.0 126.3 jit_solution(10946745416837595346)
XLA Ops:
  0.6 123.1 %sublayer.1 = (bf16[256,384]{1,0:T(8,128)(2,1)}, bf16[256,384]{1,0:T(8,128)(2,1)}, f32[576,384]{1,0:T(8,128)}, f32[192,384]{1,0:T(8,128)}) custom-call(bf16[256,3072]{1,0:T(8,128)(2,1)} %tok_hbm.1, bf16[256,3072]{1,0:T(8,128)(2,1)} %cot_hbm.1, bf16[576,384]{1,0:T(8,128)(2,1)} %bitcast.8, bf16[192,384]{1,0:T(8,128)(2,1)} %wo_hbm.1, s32[16]{0:T(128)} %slab.1, ...), custom_call_target="tpu_custom_call" | custom-call | flops 20000000000 | bytes 10000000 | tf_op jit(solution)/shard_map/sublayer/pallas_call | solution.py:929
  123.7 2.6 %deliver.1 = (bf16[256,384]{1,0:T(8,128)(2,1)}, bf16[256,384]{1,0:T(8,128)(2,1)}, f32[576,384]{1,0:T(8,128)}, f32[192,384]{1,0:T(8,128)}) custom-call(bf16[256,384]{1,0:T(8,128)(2,1)} %get-tuple-element.12.refs_0_, bf16[256,384]{1,0:T(8,128)(2,1)} %get-tuple-element.13.refs_1_, f32[576,384]{1,0:T(8,128)} %get-tuple-element.14.refs_2_, ...), custom_call_target="tpu_custom_call" | custom-call | tf_op jit(solution)/shard_map/deliver/pallas_call | solution.py:940
